TPU v7x, 128 devices: a whole 4x4x4 slice. The times are simulated.
128 devices in a mesh: seq: 32 (over x, y_lo, z), tp: 4 (over y_hi, core).
Axes of the slice: x: 4, y: 4 (y_hi: 2, y_lo: 2; y = y_hi * 2 + y_lo), z: 4, core: 2. Of those that a mesh axis runs over, the one named last changes fastest.
Arguments:
- query_heads: bfloat16 [8192, 2048], P('seq', 'tp'), may hold values from -96 to 96
- key_heads: bfloat16 [8192, 2048], P('seq', 'tp'), may hold values from -4 to 4
- value_heads: bfloat16 [8192, 2048], P('seq', 'tp'), may hold values from -6 to 6
- residual: bfloat16 [8192, 4096], P('seq'), may hold values from -64 to 64
- out_weight: bfloat16 [2048, 4096], P('tp'), may hold values from -0.125 to 0.125
- ln_gain: float32 [4096], replicated, may hold values from 0.1 to 1.9
- up_source: bfloat16 [4096, 4096], P(None, 'tp'), may hold values from -0.09375 to 0.09375
- down_source: bfloat16 [4096, 4096], P('tp'), may hold values from -0.09375 to 0.09375
- copy_gain: float32 [4096], P('tp'), may hold values from 0.3 to 3
- neuron_source: int32 [4096], P('tp'), may hold values from 0 to 4095, as said below
- cotangent: bfloat16 [8192, 4096], P('seq'), may hold values from -6 to 6
Outputs:
- encoded: float32 [8192, 4096], P(('seq', 'tp'))
- grad_query: float32 [8192, 2048], P('seq', 'tp')
- grad_key: float32 [8192, 2048], P('seq', 'tp')
- grad_value: float32 [8192, 2048], P('seq', 'tp')
- grad_residual: float32 [8192, 4096], P('seq', 'tp')
Inputs may be any that keep to these rules, and one draw needn't show every extreme that they name: Added neuron j splits a source neuron of its own group: neuron_source[j] // 1024 == j // 1024.
All inputs are finite; a program needn't handle non-finite values.
Results may differ from a plain program's by a relative error of at most 0.035.
Values may be sent and summed in bfloat16 or wider, within the bound.
No kernel may reach another device: no remote copies, remote signals or barrier semaphores. Data moves between devices by JAX's collectives and lax.ppermute only.
A program may use at most 128 MiB of HBM per device.

v0:
```python
import functools
import math

import jax
import jax.numpy as jnp
from jax import lax
from jax.experimental import pallas as pl
from jax.experimental.pallas import tpu as pltpu
from jax.sharding import PartitionSpec as P

HEAD_DIM = 128
EPSILON = 1e-05
LOG2E = math.log2(math.e)
F32 = jnp.float32
BF16 = jnp.bfloat16
NT = (((1,), (1,)), ((), ()))
STAT_ROWS = 16
VMEM_LIMIT = 16 * 1024 * 1024
OUT_STEP = 512
NORM_STEP = 512
COST = 1024

VMEM = pl.BlockSpec(memory_space=pltpu.VMEM)
SMEM = pl.BlockSpec(memory_space=pltpu.SMEM)
ANY = pl.BlockSpec(memory_space=pl.ANY)


def call(kernel, out_shape, in_specs, scratch=()):
    return pl.pallas_call(
        kernel,
        out_shape=out_shape,
        in_specs=in_specs,
        out_specs=jax.tree.map(lambda _: VMEM, out_shape),
        scratch_shapes=list(scratch),
        compiler_params=pltpu.CompilerParams(vmem_limit_bytes=VMEM_LIMIT),
        cost_estimate=pl.CostEstimate(flops=COST, bytes_accessed=COST, transcendentals=0),
    )


def shape(dims, dtype):
    return jax.ShapeDtypeStruct(dims, dtype)


def dot(a, b):
    return jnp.dot(a, b, preferred_element_type=F32)


def dot_nt(a, b):
    return lax.dot_general(a, b, NT, preferred_element_type=F32)


def swap_core(array):
    return lax.ppermute(array, "tp", [(0, 1), (1, 0), (2, 3), (3, 2)])


def swap_chip(array):
    return lax.ppermute(array, "tp", [(0, 2), (2, 0), (1, 3), (3, 1)])


def after(value, *earlier):
    return lax.optimization_barrier((value, earlier))[0]


def from_behind(array, by):
    count = lax.axis_size("seq")
    return lax.ppermute(array, "seq", [(i, i + by) for i in range(count) if 0 <= i + by < count])


def three_parts(values):
    high = values.astype(BF16).astype(F32)
    middle = (values - high).astype(BF16).astype(F32)
    low = values - high - middle
    return high, middle, low


def stat_rows(columns, heads):
    rows = columns.T[:heads]
    parts = three_parts(rows)
    fill = jnp.zeros((STAT_ROWS - 3 * heads, rows.shape[1]), F32)
    return jnp.concatenate(parts + (fill,), axis=0).astype(BF16)


def read_stat(pack, head, heads, rows):
    block = pack[rows : rows + STAT_ROWS, :rows].astype(F32)
    total = block[head : head + 1]
    for part in (1, 2):
        total = total + block[part * heads + head : part * heads + head + 1]
    return total


def local_starts(core, rows):
    slab = rows // 4
    return [(2 * part + (core if own else 1 - core)) * slab for own in (True, False) for part in range(2)]


def attention_kernel(scale, place, q_ref, k0, v0, kv_a, kv_b, kv_c, kv_d, att_ref, pack_ref, lse_ref):
    rows, width = q_ref.shape
    heads = width // HEAD_DIM
    slab = rows // 4
    seq, blocks, core = place[0], place[1], place[2]
    for index, start in enumerate(local_starts(core, rows)):
        pack_ref[index * slab : (index + 1) * slab] = q_ref[pl.ds(start, slab)]
    lane = lax.broadcasted_iota(jnp.int32, (rows, HEAD_DIM), 1)
    lse_all = jnp.zeros((rows, HEAD_DIM), F32)
    for head in range(heads):
        cols = slice(head * HEAD_DIM, (head + 1) * HEAD_DIM)
        query = pack_ref[:rows, cols]
        scores = []
        values = []
        for offset, pair in ((0, None), (-2, kv_a), (-1, kv_b), (1, kv_c), (2, kv_d)):
            key = k0[:, cols] if pair is None else pair[0, :, cols]
            values.append(v0[:, cols] if pair is None else pair[1, :, cols])
            score = dot_nt(query, key) * (scale * LOG2E)
            if pair is not None:
                valid = (seq + offset >= 0) & (seq + offset < blocks)
                score = jnp.where(valid, score, -1e30)
            scores.append(score)
        top = scores[0]
        for score in scores[1:]:
            top = jnp.maximum(top, score)
        top = jnp.max(top, axis=1, keepdims=True)
        total = jnp.zeros((rows, rows), F32)
        mixed = jnp.zeros((rows, HEAD_DIM), F32)
        for score, value in zip(scores, values):
            weight = jnp.exp2(score - top)
            total = total + weight
            mixed = mixed + dot(weight.astype(BF16), value)
        total = jnp.sum(total, axis=1, keepdims=True)
        att_ref[:, cols] = (mixed / total).astype(BF16)
        lse_all = jnp.where(lane == head, top + jnp.log2(total), lse_all)
    lse_ref[...] = lse_all
    pack_ref[rows:, :rows] = stat_rows(lse_all, heads)
    pack_ref[rows:, rows:] = jnp.zeros((STAT_ROWS, width - rows), BF16)


def out_kernel(att_ref, weight_ref, own_ref, other_ref):
    rows, width = own_ref.shape
    for start in range(0, width, OUT_STEP):
        product = dot(att_ref[...], weight_ref[:, start : start + OUT_STEP]).astype(BF16)
        own_ref[:, start : start + OUT_STEP] = product[:rows]
        other_ref[:, start : start + OUT_STEP] = product[rows:]


def lane_sums(values):
    total = values[:, :HEAD_DIM]
    for start in range(HEAD_DIM, values.shape[1], HEAD_DIM):
        total = total + values[:, start : start + HEAD_DIM]
    return total


def norm_kernel(near_ref, far_ref, residual_ref, gain_ref, unit_ref, sigma_ref, normed_ref):
    rows, width = residual_ref.shape
    spans = [slice(at, at + NORM_STEP) for at in range(0, width, NORM_STEP)]
    total = jnp.zeros((rows, HEAD_DIM), F32)
    for cols in spans:
        stream = residual_ref[:, cols].astype(F32) + near_ref[:, cols].astype(F32) + far_ref[:, cols].astype(F32)
        unit_ref[:, cols] = stream
        total = total + lane_sums(stream)
    mean = jnp.sum(total, axis=-1, keepdims=True) / width
    total = jnp.zeros((rows, HEAD_DIM), F32)
    for cols in spans:
        centered = unit_ref[:, cols] - mean
        total = total + lane_sums(centered * centered)
    sigma = jnp.sqrt(jnp.sum(total, axis=-1, keepdims=True) / width + EPSILON)
    sigma_ref[...] = jnp.broadcast_to(sigma, sigma_ref.shape)
    inverse = 1.0 / sigma
    for cols in spans:
        unit = (unit_ref[:, cols] - mean) * inverse
        unit_ref[:, cols] = unit
        normed_ref[:, cols] = (unit * gain_ref[:, cols]).astype(BF16)


def norm_back_kernel(near_ref, far_ref, cot_ref, gain_ref, unit_ref, sigma_ref, low_ref, scaled_ref):
    rows, width = cot_ref.shape
    spans = [slice(at, at + NORM_STEP) for at in range(0, width, NORM_STEP)]
    total = jnp.zeros((rows, HEAD_DIM), F32)
    total_along = jnp.zeros((rows, HEAD_DIM), F32)
    for cols in spans:
        grad = cot_ref[:, cols].astype(F32) + near_ref[:, cols].astype(F32) + far_ref[:, cols].astype(F32)
        scaled = grad * gain_ref[:, cols]
        scaled_ref[:, cols] = scaled
        total = total + lane_sums(scaled)
        total_along = total_along + lane_sums(scaled * unit_ref[:, cols])
    mean = jnp.sum(total, axis=-1, keepdims=True) / width
    along = jnp.sum(total_along, axis=-1, keepdims=True) / width
    inverse = 1.0 / sigma_ref[:, :1]
    for cols in spans:
        grad = (scaled_ref[:, cols] - mean - unit_ref[:, cols] * along) * inverse
        low_ref[:, cols] = grad.astype(BF16)


def gelu_and_slope(v):
    root = math.sqrt(2.0 / math.pi)
    square = v * v
    t = jnp.tanh(v * (root + root * 0.044715 * square))
    plus = 0.5 + 0.5 * t
    slope = plus + 0.5 * v * (1.0 - t * t) * (root + 3.0 * root * 0.044715 * square)
    return v * plus, slope


def ffn_kernel(
    own_ref, near_ref, up_ref, pick_ref, grad_ref, grad_copy_ref, inverse_ref, gain_ref, merged_ref, hidden_grad_ref
):
    rows = jnp.concatenate([own_ref[...], near_ref[...]], axis=0)
    source = dot(rows, up_ref[...])
    high = source.astype(BF16)
    low = (source - high.astype(F32)).astype(BF16)
    copied = (dot(high, pick_ref[...]) + dot(low, pick_ref[...])) * gain_ref[...]
    act_copy, slope_copy = gelu_and_slope(copied)
    act, slope = gelu_and_slope(source)
    back_copy = (grad_copy_ref[...] * slope_copy).astype(BF16)
    hidden_grad_ref[...] = (grad_ref[...] * slope + dot_nt(back_copy, pick_ref[...])).astype(BF16)
    merged = act + dot_nt(act_copy.astype(BF16), pick_ref[...])
    merged_ref[...] = (merged * inverse_ref[...]).astype(BF16)


def back_kernel(hidden_grad_ref, up_ref, own_ref, other_ref):
    rows, width = own_ref.shape
    for start in range(0, width, OUT_STEP):
        product = dot_nt(hidden_grad_ref[...], up_ref[start : start + OUT_STEP]).astype(BF16)
        own_ref[:, start : start + OUT_STEP] = product[:rows]
        other_ref[:, start : start + OUT_STEP] = product[rows:]


def grad_attended_kernel(own_ref, near_ref, weight_ref, att_ref, pack_ref, delta_ref):
    rows, width = att_ref.shape
    heads = width // HEAD_DIM
    low = jnp.concatenate([own_ref[...], near_ref[...]], axis=0)
    pack_ref[:rows] = dot_nt(low, weight_ref[...]).astype(BF16)
    product = pack_ref[:rows].astype(F32) * att_ref[...].astype(F32)
    lane = lax.broadcasted_iota(jnp.int32, (rows, HEAD_DIM), 1)
    delta = jnp.zeros((rows, HEAD_DIM), F32)
    for head in range(heads):
        part = jnp.sum(product[:, head * HEAD_DIM : (head + 1) * HEAD_DIM], axis=1, keepdims=True)
        delta = jnp.where(lane == head, part, delta)
    delta_ref[...] = delta
    pack_ref[rows:, :rows] = stat_rows(delta, heads)
    pack_ref[rows:, rows:] = jnp.zeros((STAT_ROWS, width - rows), BF16)


def grad_query_kernel(
    scale, place, q_pack, do_pack, lse_ref, delta_ref, k0, v0, kv_a, kv_b, kv_c, kv_d, grad_ref
):
    rows, width = grad_ref.shape
    heads = width // HEAD_DIM
    slab = rows // 4
    seq, blocks, core = place[0], place[1], place[2]
    for head in range(heads):
        cols = slice(head * HEAD_DIM, (head + 1) * HEAD_DIM)
        query, out_grad = q_pack[:rows, cols], do_pack[:rows, cols]
        lse, delta = lse_ref[:, head : head + 1], delta_ref[:, head : head + 1]
        total = jnp.zeros((rows, HEAD_DIM), F32)
        for offset, pair in ((0, None), (-2, kv_a), (-1, kv_b), (1, kv_c), (2, kv_d)):
            key = k0[:, cols] if pair is None else pair[0, :, cols]
            value = v0[:, cols] if pair is None else pair[1, :, cols]
            score = dot_nt(query, key) * (scale * LOG2E) - lse
            if pair is not None:
                valid = (seq + offset >= 0) & (seq + offset < blocks)
                score = jnp.where(valid, score, -1e30)
            grad_score = jnp.exp2(score) * (dot_nt(out_grad, value) - delta)
            total = total + dot(grad_score.astype(BF16), key)
        total = total * scale
        for index, start in enumerate(local_starts(core, rows)):
            grad_ref[pl.ds(start, slab), cols] = total[index * slab : (index + 1) * slab]


def grad_key_value_kernel(scale, count, start, *refs):
    packs, refs = refs[: 2 * count], refs[2 * count :]
    k0, v0 = refs[:2]
    grad_key_ref, grad_value_ref = refs[-2:]
    rows, width = k0.shape
    heads = width // HEAD_DIM
    for head in range(heads):
        cols = slice(head * HEAD_DIM, (head + 1) * HEAD_DIM)
        key, value = k0[:, cols], v0[:, cols]
        grad_key = jnp.zeros((rows, HEAD_DIM), F32)
        grad_value = jnp.zeros((rows, HEAD_DIM), F32)
        for index in range(count):
            q_pack, do_pack = packs[2 * index], packs[2 * index + 1]
            query, out_grad = q_pack[:rows, cols], do_pack[:rows, cols]
            score = dot_nt(key, query) * (scale * LOG2E) - read_stat(q_pack, head, heads, rows)
            weight = jnp.exp2(score)
            grad_value = grad_value + dot(weight.astype(BF16), out_grad)
            grad_score = weight * (dot_nt(value, out_grad) - read_stat(do_pack, head, heads, rows))
            grad_key = grad_key + dot(grad_score.astype(BF16), query)
        grad_key = grad_key * scale
        if not start:
            grad_key = grad_key + refs[2][:, cols]
            grad_value = grad_value + refs[3][:, cols]
        grad_key_ref[:, cols] = grad_key
        grad_value_ref[:, cols] = grad_value


def shards(
    query_heads,
    key_heads,
    value_heads,
    residual,
    out_weight,
    ln_gain,
    up_source,
    down_source,
    copy_gain,
    neuron_source,
    cotangent,
):
    rows, head_width = query_heads.shape
    model_width = residual.shape[1]
    src_width = up_source.shape[1]
    half = rows // 2
    scale = 1.0 / math.sqrt(HEAD_DIM)
    seq = lax.axis_index("seq")
    blocks = lax.axis_size("seq")
    tp_place = lax.axis_index("tp")
    core, chip = tp_place % 2, tp_place // 2
    place = jnp.stack([seq, jnp.full_like(seq, blocks), core]).astype(jnp.int32)

    kv = jnp.stack([key_heads, value_heads])
    behind1 = from_behind(kv, 1)
    ahead1 = from_behind(kv, -1)

    def half_rows(array, place):
        split = array.reshape(2, 2, half // 2, array.shape[1])
        return lax.dynamic_slice_in_dim(split, place, 1, 1).reshape(half, array.shape[1])

    cot_own = half_rows(cotangent, core)
    cot_local = jnp.concatenate([cot_own, half_rows(cotangent, 1 - core)], axis=0)
    grad_merged = dot_nt(cot_local, down_source)
    behind1, ahead1, grad_merged = lax.optimization_barrier((behind1, ahead1, grad_merged))
    behind2 = from_behind(behind1, 1)
    ahead2 = from_behind(ahead1, -1)

    residual_own = half_rows(residual, core)
    local_source = neuron_source - tp_place * src_width
    pick = (lax.broadcasted_iota(jnp.int32, (src_width, src_width), 0) == local_source[None, :])
    counts = 1.0 + jnp.sum(pick.astype(F32), axis=1)
    pick = pick.astype(BF16)
    inverse = 1.0 / counts
    grad_merged = grad_merged * inverse
    grad_high = grad_merged.astype(BF16)
    grad_rest = (grad_merged - grad_high.astype(F32)).astype(BF16)
    grad_copy = (dot(grad_high, pick) + dot(grad_rest, pick)) * copy_gain
    gain_row = ln_gain.reshape(1, model_width)
    inverse_row = inverse.reshape(1, src_width)
    copy_row = copy_gain.reshape(1, src_width)
    behind2, ahead2, pick, grad_merged, grad_copy, residual_own = lax.optimization_barrier(
        (behind2, ahead2, pick, grad_merged, grad_copy, residual_own)
    )
    window = (key_heads, value_heads, behind2, behind1, ahead1, ahead2)

    attended, q_pack, lse = call(
        functools.partial(attention_kernel, scale),
        (
            shape((rows, head_width), BF16),
            shape((rows + STAT_ROWS, head_width), BF16),
            shape((rows, HEAD_DIM), F32),
        ),
        [SMEM] + [VMEM] * 7,
    )(place, query_heads, *window)

    def chip_sum(kernel, operands, beside):
        own, other = call(kernel, (shape((half, model_width), BF16),) * 2, [VMEM, VMEM])(*operands)
        other, beside = lax.optimization_barrier((swap_core(other), beside))
        near = (own.astype(F32) + other.astype(F32)).astype(BF16)
        return near, swap_chip(near), beside

    near, far, _ = chip_sum(out_kernel, (attended, out_weight), ())

    q_early = after(q_pack, near)
    q_packs = {offset: from_behind(q_early, -offset) for offset in (-1, 1, -2, 2)}
    far, q_packs = lax.optimization_barrier((far, q_packs))

    unit, sigma, normed = call(
        norm_kernel,
        (
            shape((half, model_width), F32),
            shape((half, HEAD_DIM), F32),
            shape((half, model_width), BF16),
        ),
        [VMEM] * 4,
    )(near, far, residual_own, gain_row)
    near_normed = swap_core(normed)
    merged, hidden_grad = call(ffn_kernel, (shape((rows, src_width), BF16),) * 2, [VMEM] * 8)(
        normed, near_normed, up_source, pick, grad_merged, grad_copy, inverse_row, copy_row
    )
    ffn_part = dot(merged, down_source).astype(BF16)
    near, far, ffn_part = chip_sum(back_kernel, (hidden_grad, up_source), ffn_part)
    ffn_near = swap_core(ffn_part[half:])
    ffn_chip = (ffn_part[:half].astype(F32) + ffn_near.astype(F32)).reshape(2, half // 2, model_width)
    ffn_send = jnp.where(chip == 0, ffn_chip[1], ffn_chip[0]).astype(BF16)
    ffn_mine = jnp.where(chip == 0, ffn_chip[0], ffn_chip[1])
    far, ffn_send, ffn_mine = lax.optimization_barrier((far, ffn_send, ffn_mine))

    low = call(
        norm_back_kernel,
        shape((half, model_width), BF16),
        [VMEM] * 6,
        scratch=[pltpu.VMEM((half, model_width), F32)],
    )(near, far, cot_own, gain_row, unit, sigma)
    near_low = swap_core(low)
    do_pack, delta = call(
        grad_attended_kernel,
        (shape((rows + STAT_ROWS, head_width), BF16), shape((rows, HEAD_DIM), F32)),
        [VMEM] * 4,
    )(low, near_low, out_weight, attended)

    do_packs = {offset: from_behind(do_pack, -offset) for offset in (-2, 2, -1, 1)}

    ffn_far = swap_chip(after(ffn_send, do_pack))

    grad_query = call(
        functools.partial(grad_query_kernel, scale),
        shape((rows, head_width), F32),
        [SMEM] + [VMEM] * 10,
    )(place, q_pack, do_pack, lse, delta, *window)

    def grad_key_value(pairs, sums):
        return call(
            functools.partial(grad_key_value_kernel, scale, len(pairs), not sums),
            (shape((rows, head_width), F32),) * 2,
            [VMEM] * (2 * len(pairs) + 2 + len(sums)),
        )(*[pack for pair in pairs for pack in pair], key_heads, value_heads, *sums)

    sums = grad_key_value(
        [(q_pack, do_pack)] + [(q_packs[offset], do_packs[offset]) for offset in (-1, 1)], ()
    )
    own_unit = lax.dynamic_slice_in_dim(unit, chip * (half // 2), half // 2, 0)
    encoded = own_unit * ln_gain + (ffn_mine + ffn_far.astype(F32))
    far_pairs = [(q_packs[offset], do_packs[offset]) for offset in (-2, 2)]
    grad_key, grad_value = grad_key_value(far_pairs, sums)

    col_width = model_width // lax.axis_size("tp")
    first = jnp.where(core == 0, low, near_low).reshape(2, half // 2, model_width)
    second = jnp.where(core == 0, near_low, low).reshape(2, half // 2, model_width)
    low_all = jnp.stack([first, second], axis=1).reshape(rows, model_width)
    grad_residual = lax.dynamic_slice_in_dim(low_all, tp_place * col_width, col_width, 1).astype(F32)
    return (encoded, grad_query, grad_key, grad_value, grad_residual)


def solution(mesh):
    in_specs = (
        P("seq", "tp"),
        P("seq", "tp"),
        P("seq", "tp"),
        P("seq", None),
        P("tp", None),
        P(),
        P(None, "tp"),
        P("tp", None),
        P("tp"),
        P("tp"),
        P("seq", None),
    )
    out_specs = (
        P(("seq", "tp"), None),
        P("seq", "tp"),
        P("seq", "tp"),
        P("seq", "tp"),
        P("seq", "tp"),
    )
    return jax.shard_map(shards, mesh=mesh, in_specs=in_specs, out_specs=out_specs, check_vma=False)
```

profile of v0, /device:TPU:109, one launch (start us, length us, event | category | flops | bytes accessed | tf_op | source)
XLA Modules:
  0.0 187.4 jit_solution(542797268346829590)
XLA Ops:
  0.6 1.2 pad_maximum_fusion.1
  1.9 2.0 %collective-permute-start.1 = (bf16[2,256,512]{2,1,0:T(8,128)(2,1)S(1)}, bf16[2,256,512]{2,1,0:T(8,128)(2,1)S(1)}, u32[]{:S(2)}, u32[]{:S(2)}) collective-permute-start(bf16[2,256,512]{2,1,0:T(8,128)(2,1)S(1)} %pad_maximum_fusion.1), channel_id=1, source_target_pairs={{4,0},{8,4},{12,8},{16,12},{20,16},{24,20},{28,24},{32,28},{36,32}... | collective-permute-start | bytes 1572872 | tf_op jit(solution)/shard_map/ppermute | solution.py:66
  3.9 6.3 %collective-permute-start = (bf16[2,256,512]{2,1,0:T(8,128)(2,1)S(1)}, bf16[2,256,512]{2,1,0:T(8,128)(2,1)}, u32[]{:S(2)}, u32[]{:S(2)}) collective-permute-start(bf16[2,256,512]{2,1,0:T(8,128)(2,1)S(1)} %pad_maximum_fusion.1), channel_id=1, source_target_pairs={{0,4},{4,8},{8,12},{12,16},{16,20},{20,24},{24,28},{28,32},{32,36}... | collective-permute-start | bytes 1572872 | tf_op jit(solution)/shard_map/ppermute | solution.py:66
  11.4 2.2 %fusion.2.pick_ref = bf16[1024,1024]{1,0:T(8,128)(2,1)} fusion(s32[1024]{0:T(1024)S(1)} %broadcast_subtract_fusion), kind=kLoop, calls=%fused_computation.5 | loop fusion | flops 2097152 | bytes 2101248 | tf_op jit(solution)/shard_map/convert_element_type | solution.py:337
  13.6 1.7 constant_dynamic-slice_fusion.2
  15.3 6.1 %fusion.3 = f32[256,1024]{1,0:T(8,128)S(1)} fusion(bf16[1024,4096]{1,0:T(8,128)(2,1)} %param.18, bf16[128,4096]{1,0:T(8,128)(2,1)S(1)} %bitcast.40, bf16[128,4096]{1,0:T(8,128)(2,1)S(1)} %bitcast.29), kind=kOutput, calls=%fused_computation.6 | convolution fusion | flops 2151677952 | bytes 11534336 | tf_op jit(solution)/shard_map/dot_general | solution.py:49
  21.6 6.0 %collective-permute-start.2 = (bf16[2,256,512]{2,1,0:T(8,128)(2,1)}, bf16[2,256,512]{2,1,0:T(8,128)(2,1)S(1)}, u32[]{:S(2)}, u32[]{:S(2)}) collective-permute-start(bf16[2,256,512]{2,1,0:T(8,128)(2,1)} %collective-permute-done.kv_b), channel_id=1, source_target_pairs={{0,4},{4,8},{8,12},{12,16},{16,20},{20,24},{24,28},{28,32},{32,36}... | collective-permute-start | bytes 1572872 | tf_op jit(solution)/shard_map/ppermute | solution.py:66
  27.7 1.9 %collective-permute-start.3 = (bf16[2,256,512]{2,1,0:T(8,128)(2,1)S(1)}, bf16[2,256,512]{2,1,0:T(8,128)(2,1)S(1)}, u32[]{:S(2)}, u32[]{:S(2)}) collective-permute-start(bf16[2,256,512]{2,1,0:T(8,128)(2,1)S(1)} %collective-permute-done.1.kv_c), channel_id=1, source_target_pairs={{4,0},{8,4},{12,8},{16,12},{20,16},{24,20},{28,24},{32,28},{36,32}... | collective-permute-start | bytes 1572872 | tf_op jit(solution)/shard_map/ppermute | solution.py:66
  31.9 5.4 %collective-permute-done.2.kv_a = bf16[2,256,512]{2,1,0:T(8,128)(2,1)S(1)} collective-permute-done((bf16[2,256,512]{2,1,0:T(8,128)(2,1)}, bf16[2,256,512]{2,1,0:T(8,128)(2,1)S(1)}, u32[]{:S(2)}, u32[]{:S(2)}) %collective-permute-start.2) | collective-permute-done | bytes 524320 | tf_op jit(solution)/shard_map/ppermute | solution.py:66
  37.3 6.5 %collective-permute-done.3.kv_d = bf16[2,256,512]{2,1,0:T(8,128)(2,1)S(1)} collective-permute-done((bf16[2,256,512]{2,1,0:T(8,128)(2,1)S(1)}, bf16[2,256,512]{2,1,0:T(8,128)(2,1)S(1)}, u32[]{:S(2)}, u32[]{:S(2)}) %collective-permute-start.3) | collective-permute-done | bytes 524320 | tf_op jit(solution)/shard_map/ppermute | solution.py:66
  43.8 3.6 %shard_map.146 = (bf16[256,512]{1,0:T(8,128)(2,1)S(1)}, bf16[272,512]{1,0:T(8,128)(2,1)S(1)}, f32[256,128]{1,0:T(8,128)S(1)}) custom-call(s32[3]{0:T(128)S(1)} %pad_add_fusion.place, bf16[256,512]{1,0:T(8,128)(2,1)S(1)} %copy-done.26, bf16[256,512]{1,0:T(8,128)(2,1)S(1)} %copy-done.5, bf16[256,512]{1,0:T(8,128)(2,1)S(1)} %copy-done.6, ...), custom_call_target="tpu_custom_call" | custom-call | flops 1024 | bytes 1024 | tf_op jit(solution)/shard_map/pallas_call | solution.py:351
  48.3 1.3 shard_map.147
  49.6 3.1 %collective-permute-start.4 = (bf16[128,4096]{1,0:T(8,128)(2,1)S(1)}, bf16[128,4096]{1,0:T(8,128)(2,1)S(1)}, u32[]{:S(2)}, u32[]{:S(2)}) collective-permute-start(bf16[128,4096]{1,0:T(8,128)(2,1)S(1)} %get-tuple-element.51), channel_id=1, source_target_pairs={{0,1},{1,0},{2,3},{3,2},{4,5},{5,4},{6,7},{7,6},{8,9},{9,8},{10,11... | collective-permute-start | bytes 3145736 | tf_op jit(solution)/shard_map/ppermute | solution.py:53
  52.8 2.3 %collective-permute-done.4 = bf16[128,4096]{1,0:T(8,128)(2,1)S(1)} collective-permute-done((bf16[128,4096]{1,0:T(8,128)(2,1)S(1)}, bf16[128,4096]{1,0:T(8,128)(2,1)S(1)}, u32[]{:S(2)}, u32[]{:S(2)}) %collective-permute-start.4) | collective-permute-done | bytes 1048608 | tf_op jit(solution)/shard_map/ppermute | solution.py:53
  55.3 2.1 %collective-permute-start.5 = (bf16[128,4096]{1,0:T(8,128)(2,1)S(1)}, bf16[128,4096]{1,0:T(8,128)(2,1)S(1)}, u32[]{:S(2)}, u32[]{:S(2)}) collective-permute-start(bf16[128,4096]{1,0:T(8,128)(2,1)S(1)} %add_convert_fusion.1.near_ref), channel_id=1, source_target_pairs={{0,2},{2,0},{1,3},{3,1},{4,6},{6,4},{5,7},{7,5},{8,10},{10,8},{9,1... | collective-permute-start | bytes 3145736 | tf_op jit(solution)/shard_map/ppermute | solution.py:57
  57.4 1.9 %collective-permute-start.9 = (bf16[272,512]{1,0:T(8,128)(2,1)S(1)}, bf16[272,512]{1,0:T(8,128)(2,1)S(1)}, u32[]{:S(2)}, u32[]{:S(2)}) collective-permute-start(bf16[272,512]{1,0:T(8,128)(2,1)S(1)} %get-tuple-element.53.q_pack.refs_0_), channel_id=1, source_target_pairs={{8,0},{12,4},{16,8},{20,12},{24,16},{28,20},{32,24},{36,28},{40,32... | collective-permute-start | bytes 835592 | tf_op jit(solution)/shard_map/ppermute | solution.py:66
  59.3 1.9 %collective-permute-start.8 = (bf16[272,512]{1,0:T(8,128)(2,1)S(1)}, bf16[272,512]{1,0:T(8,128)(2,1)S(1)}, u32[]{:S(2)}, u32[]{:S(2)}) collective-permute-start(bf16[272,512]{1,0:T(8,128)(2,1)S(1)} %get-tuple-element.53.q_pack.refs_0_), channel_id=1, source_target_pairs={{4,0},{8,4},{12,8},{16,12},{20,16},{24,20},{28,24},{32,28},{36,32}... | collective-permute-start | bytes 835592 | tf_op jit(solution)/shard_map/ppermute | solution.py:66
  61.3 6.4 %collective-permute-start.7 = (bf16[272,512]{1,0:T(8,128)(2,1)S(1)}, bf16[272,512]{1,0:T(8,128)(2,1)S(1)}, u32[]{:S(2)}, u32[]{:S(2)}) collective-permute-start(bf16[272,512]{1,0:T(8,128)(2,1)S(1)} %get-tuple-element.53.q_pack.refs_0_), channel_id=1, source_target_pairs={{0,4},{4,8},{8,12},{12,16},{16,20},{20,24},{24,28},{28,32},{32,36}... | collective-permute-start | bytes 835592 | tf_op jit(solution)/shard_map/ppermute | solution.py:66
  67.6 3.8 %collective-permute-start.6 = (bf16[272,512]{1,0:T(8,128)(2,1)S(1)}, bf16[272,512]{1,0:T(8,128)(2,1)S(1)}, u32[]{:S(2)}, u32[]{:S(2)}) collective-permute-start(bf16[272,512]{1,0:T(8,128)(2,1)S(1)} %get-tuple-element.53.q_pack.refs_0_), channel_id=1, source_target_pairs={{0,8},{4,12},{8,16},{12,20},{16,24},{20,28},{24,32},{28,36},{32,40... | collective-permute-start | bytes 835592 | tf_op jit(solution)/shard_map/ppermute | solution.py:66
  72.5 5.0 %collective-permute-done.8.refs_4_ = bf16[272,512]{1,0:T(8,128)(2,1)S(1)} collective-permute-done((bf16[272,512]{1,0:T(8,128)(2,1)S(1)}, bf16[272,512]{1,0:T(8,128)(2,1)S(1)}, u32[]{:S(2)}, u32[]{:S(2)}) %collective-permute-start.8) | collective-permute-done | bytes 278560 | tf_op jit(solution)/shard_map/ppermute | solution.py:66
  77.5 4.7 %collective-permute-done.6.refs_0_ = bf16[272,512]{1,0:T(8,128)(2,1)S(1)} collective-permute-done((bf16[272,512]{1,0:T(8,128)(2,1)S(1)}, bf16[272,512]{1,0:T(8,128)(2,1)S(1)}, u32[]{:S(2)}, u32[]{:S(2)}) %collective-permute-start.6) | collective-permute-done | bytes 278560 | tf_op jit(solution)/shard_map/ppermute | solution.py:66
  82.2 11.0 %collective-permute-done.5.far_ref = bf16[128,4096]{1,0:T(8,128)(2,1)S(1)} collective-permute-done((bf16[128,4096]{1,0:T(8,128)(2,1)S(1)}, bf16[128,4096]{1,0:T(8,128)(2,1)S(1)}, u32[]{:S(2)}, u32[]{:S(2)}) %collective-permute-start.5) | collective-permute-done | bytes 1048608 | tf_op jit(solution)/shard_map/ppermute | solution.py:57
  93.2 1.2 shard_map.148
  94.4 1.3 collective-permute-start.10
  95.7 2.3 %collective-permute-done.10.near_ref = bf16[128,4096]{1,0:T(8,128)(2,1)S(1)} collective-permute-done((bf16[128,4096]{1,0:T(8,128)(2,1)S(1)}, bf16[128,4096]{1,0:T(8,128)(2,1)S(1)}, u32[]{:S(2)}, u32[]{:S(2)}) %collective-permute-start.10) | collective-permute-done | bytes 1048608 | tf_op jit(solution)/shard_map/ppermute | solution.py:53
  98.0 4.8 %shard_map.149 = (bf16[256,1024]{1,0:T(8,128)(2,1)S(1)}, bf16[256,1024]{1,0:T(8,128)(2,1)S(1)}) custom-call(bf16[128,4096]{1,0:T(8,128)(2,1)S(1)} %get-tuple-element.57.own_ref, bf16[128,4096]{1,0:T(8,128)(2,1)S(1)} %collective-permute-done.10.near_ref, bf16[4096,1024]{1,0:T(8,128)(2,1)S(1)} %bitcast.26, bf16[1024,1024]{1,0:T(8,128)(2,1)S(1)} %copy-done.4, ...), custom_call_target="tpu_custom_call" | custom-call | flops 1024 | bytes 1024 | tf_op jit(solution)/shard_map/pallas_call | solution.py:383
  102.8 2.4 %shard_map.150 = (bf16[128,4096]{1,0:T(8,128)(2,1)S(1)}, bf16[128,4096]{1,0:T(8,128)(2,1)S(1)}) custom-call(bf16[256,1024]{1,0:T(8,128)(2,1)S(1)} %get-tuple-element.61.hidden_grad_ref, bf16[4096,1024]{1,0:T(8,128)(2,1)S(1)} %bitcast.26), custom_call_target="tpu_custom_call" | custom-call | flops 1024 | bytes 1024 | tf_op jit(solution)/shard_map/pallas_call | solution.py:362
  105.7 2.4 %convolution_convert_fusion = bf16[256,4096]{1,0:T(8,128)(2,1)S(1)} fusion(bf16[256,1024]{1,0:T(8,128)(2,1)S(1)} %get-tuple-element.64, bf16[1024,4096]{1,0:T(8,128)(2,1)S(1)} %bitcast.42), kind=kOutput, calls=%fused_computation | convolution fusion | flops 2148532224 | bytes 11010048 | tf_op jit(solution)/shard_map/dot_general | solution.py:45
  108.1 1.3 copy-done.32
  110.6 1.6 add_convert_fusion.near_ref
  112.2 2.3 %collective-permute-start.12 = (bf16[128,4096]{1,0:T(8,128)(2,1)S(1)}, bf16[128,4096]{1,0:T(8,128)(2,1)S(1)}, u32[]{:S(2)}, u32[]{:S(2)}) collective-permute-start(bf16[128,4096]{1,0:T(8,128)(2,1)S(1)} %add_convert_fusion.near_ref), channel_id=1, source_target_pairs={{0,2},{2,0},{1,3},{3,1},{4,6},{6,4},{5,7},{7,5},{8,10},{10,8},{9,1... | collective-permute-start | bytes 3145736 | tf_op jit(solution)/shard_map/ppermute | solution.py:57
  114.5 1.5 convert_add_fusion
  118.0 20.4 %collective-permute-done.12.far_ref = bf16[128,4096]{1,0:T(8,128)(2,1)S(1)} collective-permute-done((bf16[128,4096]{1,0:T(8,128)(2,1)S(1)}, bf16[128,4096]{1,0:T(8,128)(2,1)S(1)}, u32[]{:S(2)}, u32[]{:S(2)}) %collective-permute-start.12) | collective-permute-done | bytes 1048608 | tf_op jit(solution)/shard_map/ppermute | solution.py:57
  138.3 1.3 shard_map.151.own_ref
  139.7 1.3 collective-permute-start.14
  141.0 2.3 %collective-permute-done.14.near_ref = bf16[128,4096]{1,0:T(8,128)(2,1)S(1)} collective-permute-done((bf16[128,4096]{1,0:T(8,128)(2,1)S(1)}, bf16[128,4096]{1,0:T(8,128)(2,1)S(1)}, u32[]{:S(2)}, u32[]{:S(2)}) %collective-permute-start.14) | collective-permute-done | bytes 1048608 | tf_op jit(solution)/shard_map/ppermute | solution.py:53
  143.3 2.2 %copy-done.3 = bf16[512,4096]{1,0:T(8,128)(2,1)S(1)} copy-done((bf16[512,4096]{1,0:T(8,128)(2,1)S(1)}, bf16[512,4096]{1,0:T(8,128)(2,1)}, u32[]{:S(2)}) %copy-start.3) | copy-done | bytes 4194328
  146.4 1.5 shard_map.152
  147.9 1.9 %collective-permute-start.19 = (bf16[272,512]{1,0:T(8,128)(2,1)S(1)}, bf16[272,512]{1,0:T(8,128)(2,1)S(1)}, u32[]{:S(2)}, u32[]{:S(2)}) collective-permute-start(bf16[272,512]{1,0:T(8,128)(2,1)S(1)} %get-tuple-element.71.do_pack.refs_1_), channel_id=1, source_target_pairs={{4,0},{8,4},{12,8},{16,12},{20,16},{24,20},{28,24},{32,28},{36,32}... | collective-permute-start | bytes 835592 | tf_op jit(solution)/shard_map/ppermute | solution.py:66
  149.8 6.4 %collective-permute-start.18 = (bf16[272,512]{1,0:T(8,128)(2,1)S(1)}, bf16[272,512]{1,0:T(8,128)(2,1)S(1)}, u32[]{:S(2)}, u32[]{:S(2)}) collective-permute-start(bf16[272,512]{1,0:T(8,128)(2,1)S(1)} %get-tuple-element.71.do_pack.refs_1_), channel_id=1, source_target_pairs={{0,4},{4,8},{8,12},{12,16},{16,20},{20,24},{24,28},{28,32},{32,36}... | collective-permute-start | bytes 835592 | tf_op jit(solution)/shard_map/ppermute | solution.py:66
  156.2 2.6 %collective-permute-start.17 = (bf16[272,512]{1,0:T(8,128)(2,1)S(1)}, bf16[272,512]{1,0:T(8,128)(2,1)S(1)}, u32[]{:S(2)}, u32[]{:S(2)}) collective-permute-start(bf16[272,512]{1,0:T(8,128)(2,1)S(1)} %get-tuple-element.71.do_pack.refs_1_), channel_id=1, source_target_pairs={{8,0},{12,4},{16,8},{20,12},{24,16},{28,20},{32,24},{36,28},{40,32... | collective-permute-start | bytes 835592 | tf_op jit(solution)/shard_map/ppermute | solution.py:66
  158.7 6.0 %collective-permute-start.16 = (bf16[272,512]{1,0:T(8,128)(2,1)S(1)}, bf16[272,512]{1,0:T(8,128)(2,1)S(1)}, u32[]{:S(2)}, u32[]{:S(2)}) collective-permute-start(bf16[272,512]{1,0:T(8,128)(2,1)S(1)} %get-tuple-element.71.do_pack.refs_1_), channel_id=1, source_target_pairs={{0,8},{4,12},{8,16},{12,20},{16,24},{20,28},{24,32},{28,36},{32,40... | collective-permute-start | bytes 835592 | tf_op jit(solution)/shard_map/ppermute | solution.py:66
  164.8 2.1 %collective-permute-start.15 = (bf16[64,4096]{1,0:T(8,128)(2,1)S(1)}, bf16[64,4096]{1,0:T(8,128)(2,1)S(1)}, u32[]{:S(2)}, u32[]{:S(2)}) collective-permute-start(bf16[64,4096]{1,0:T(8,128)(2,1)S(1)} %copy-done.35), channel_id=1, source_target_pairs={{0,2},{2,0},{1,3},{3,1},{4,6},{6,4},{5,7},{7,5},{8,10},{10,8},{9,1... | collective-permute-start | bytes 1572872 | tf_op jit(solution)/shard_map/ppermute | solution.py:57
  168.2 5.4 %shard_map.153 = f32[256,512]{1,0:T(8,128)} custom-call(s32[3]{0:T(128)S(1)} %pad_add_fusion.place, bf16[272,512]{1,0:T(8,128)(2,1)S(1)} %get-tuple-element.53.q_pack.refs_0_, bf16[272,512]{1,0:T(8,128)(2,1)S(1)} %get-tuple-element.71.do_pack.refs_1_, f32[256,128]{1,0:T(8,128)S(1)} %copy-done.29, f32[256,128]{1,0:T(8,128)S(1)} %get-tuple-element.74.delta_ref, ...), custom_call_target="tpu_custom_call" | custom-call | flops 1024 | bytes 1024 | tf_op jit(solution)/shard_map/pallas_call | solution.py:411
  175.0 2.7 %shard_map.154 = (f32[256,512]{1,0:T(8,128)S(1)}, f32[256,512]{1,0:T(8,128)S(1)}) custom-call(bf16[272,512]{1,0:T(8,128)(2,1)S(1)} %get-tuple-element.53.q_pack.refs_0_, bf16[272,512]{1,0:T(8,128)(2,1)S(1)} %get-tuple-element.71.do_pack.refs_1_, bf16[272,512]{1,0:T(8,128)(2,1)S(1)} %copy-done.21, bf16[272,512]{1,0:T(8,128)(2,1)S(1)} %collective-permute-done.18.refs_3_, ...), custom_call_target="tpu_custom_call" | custom-call | flops 1024 | bytes 1024 | tf_op jit(solution)/shard_map/pallas_call | solution.py:418
  177.7 2.8 %shard_map.155 = (f32[256,512]{1,0:T(8,128)}, f32[256,512]{1,0:T(8,128)}) custom-call(bf16[272,512]{1,0:T(8,128)(2,1)S(1)} %copy-done.25, bf16[272,512]{1,0:T(8,128)(2,1)S(1)} %collective-permute-done.16.refs_1_, bf16[272,512]{1,0:T(8,128)(2,1)S(1)} %copy-done.23, bf16[272,512]{1,0:T(8,128)(2,1)S(1)} %collective-permute-done.17.refs_3_, ...), custom_call_target="tpu_custom_call" | custom-call | flops 1024 | bytes 1024 | tf_op jit(solution)/shard_map/pallas_call | solution.py:418
  180.5 5.8 %collective-permute-done.15 = bf16[64,4096]{1,0:T(8,128)(2,1)S(1)} collective-permute-done((bf16[64,4096]{1,0:T(8,128)(2,1)S(1)}, bf16[64,4096]{1,0:T(8,128)(2,1)S(1)}, u32[]{:S(2)}, u32[]{:S(2)}) %collective-permute-start.15) | collective-permute-done | bytes 524320 | tf_op jit(solution)/shard_map/ppermute | solution.py:57
  186.3 1.2 add_add_fusion
  (108 shorter events, 13.0 us)
Async XLA Ops:
  0.6 20.9 %copy-start = (bf16[256,4096]{1,0:T(8,128)(2,1)S(1)}, bf16[256,4096]{1,0:T(8,128)(2,1)}, u32[]{:S(2)}) copy-start(bf16[256,4096]{1,0:T(8,128)(2,1)} %param.14) | copy-start | bytes 6291460
  1.9 19.8 %collective-permute-start.1 = (bf16[2,256,512]{2,1,0:T(8,128)(2,1)S(1)}, bf16[2,256,512]{2,1,0:T(8,128)(2,1)S(1)}, u32[]{:S(2)}, u32[]{:S(2)}) collective-permute-start(bf16[2,256,512]{2,1,0:T(8,128)(2,1)S(1)} %pad_maximum_fusion.1), channel_id=1, source_target_pairs={{4,0},{8,4},{12,8},{16,12},{20,16},{24,20},{28,24},{32,28},{36,32}... | collective-permute-start | bytes 1572872 | tf_op jit(solution)/shard_map/ppermute | solution.py:66
  3.9 17.7 %collective-permute-start = (bf16[2,256,512]{2,1,0:T(8,128)(2,1)S(1)}, bf16[2,256,512]{2,1,0:T(8,128)(2,1)}, u32[]{:S(2)}, u32[]{:S(2)}) collective-permute-start(bf16[2,256,512]{2,1,0:T(8,128)(2,1)S(1)} %pad_maximum_fusion.1), channel_id=1, source_target_pairs={{0,4},{4,8},{8,12},{12,16},{16,20},{20,24},{24,28},{28,32},{32,36}... | collective-permute-start | bytes 1572872 | tf_op jit(solution)/shard_map/ppermute | solution.py:66
  15.3 6.1 %copy-start.10 = (bf16[2,1,64,4096]{3,2,1,0:T(8,128)(2,1)}, bf16[2,1,64,4096]{3,2,1,0:T(8,128)(2,1)S(1)}, u32[]{:S(2)}) copy-start(bf16[2,1,64,4096]{3,2,1,0:T(8,128)(2,1)S(1)} %get-tuple-element.85) | copy-start | bytes 3145732
  21.6 15.7 %collective-permute-start.2 = (bf16[2,256,512]{2,1,0:T(8,128)(2,1)}, bf16[2,256,512]{2,1,0:T(8,128)(2,1)S(1)}, u32[]{:S(2)}, u32[]{:S(2)}) collective-permute-start(bf16[2,256,512]{2,1,0:T(8,128)(2,1)} %collective-permute-done.kv_b), channel_id=1, source_target_pairs={{0,4},{4,8},{8,12},{12,16},{16,20},{20,24},{24,28},{28,32},{32,36}... | collective-permute-start | bytes 1572872 | tf_op jit(solution)/shard_map/ppermute | solution.py:66
  27.7 16.2 %collective-permute-start.3 = (bf16[2,256,512]{2,1,0:T(8,128)(2,1)S(1)}, bf16[2,256,512]{2,1,0:T(8,128)(2,1)S(1)}, u32[]{:S(2)}, u32[]{:S(2)}) collective-permute-start(bf16[2,256,512]{2,1,0:T(8,128)(2,1)S(1)} %collective-permute-done.1.kv_c), channel_id=1, source_target_pairs={{4,0},{8,4},{12,8},{16,12},{20,16},{24,20},{28,24},{32,28},{36,32}... | collective-permute-start | bytes 1572872 | tf_op jit(solution)/shard_map/ppermute | solution.py:66
  29.7 14.1 %copy-start.5 = (bf16[256,512]{1,0:T(8,128)(2,1)S(1)}, bf16[256,512]{1,0:T(8,128)(2,1)}, u32[]{:S(2)}) copy-start(bf16[256,512]{1,0:T(8,128)(2,1)} %refs_4_.1) | copy-start | bytes 786436
  29.7 14.1 %copy-start.6 = (bf16[256,512]{1,0:T(8,128)(2,1)S(1)}, bf16[256,512]{1,0:T(8,128)(2,1)}, u32[]{:S(2)}) copy-start(bf16[256,512]{1,0:T(8,128)(2,1)} %refs_5_.1) | copy-start | bytes 786436
  29.7 14.1 %copy-start.26 = (bf16[256,512]{1,0:T(8,128)(2,1)S(1)}, bf16[256,512]{1,0:T(8,128)(2,1)}, u32[]{:S(2)}) copy-start(bf16[256,512]{1,0:T(8,128)(2,1)} %q_ref.1) | copy-start | bytes 786436
  29.8 18.5 %copy-start.2 = (bf16[512,4096]{1,0:T(8,128)(2,1)S(1)}, bf16[512,4096]{1,0:T(8,128)(2,1)}, u32[]{:S(2)}) copy-start(bf16[512,4096]{1,0:T(8,128)(2,1)} %weight_ref.3) | copy-start | bytes 12582916
  30.9 67.1 %slice-start = ((s8[8388608]{0:T(1024)(128)(4,1)}), s8[4194304]{0:T(1024)(128)(4,1)S(1)}, s32[]{:S(2)}) async-start(s8[8388608]{0:T(1024)(128)(4,1)} %bitcast.25), calls=%async_computation | async-start | bytes 8388608
  37.3 12.3 %copy-start.12 = (bf16[2,256,512]{2,1,0:T(8,128)(2,1)}, bf16[2,256,512]{2,1,0:T(8,128)(2,1)S(1)}, u32[]{:S(2)}) copy-start(bf16[2,256,512]{2,1,0:T(8,128)(2,1)S(1)} %collective-permute-done.2.kv_a) | copy-start | bytes 1572868
  48.3 49.7 %slice-start.1 = ((s8[8388608]{0:T(1024)(128)(4,1)}), s8[4194304]{0:T(1024)(128)(4,1)S(1)}, s32[]{:S(2)}) async-start(s8[8388608]{0:T(1024)(128)(4,1)} %bitcast.25), calls=%async_computation.1 | async-start | bytes 8388608
  49.6 43.6 %copy-start.27 = (f32[4096]{0:T(1024)S(1)}, f32[4096]{0:T(1024)}, u32[]{:S(2)}) copy-start(f32[4096]{0:T(1024)} %param.16) | copy-start | bytes 49156
  49.6 5.4 %collective-permute-start.4 = (bf16[128,4096]{1,0:T(8,128)(2,1)S(1)}, bf16[128,4096]{1,0:T(8,128)(2,1)S(1)}, u32[]{:S(2)}, u32[]{:S(2)}) collective-permute-start(bf16[128,4096]{1,0:T(8,128)(2,1)S(1)} %get-tuple-element.51), channel_id=1, source_target_pairs={{0,1},{1,0},{2,3},{3,2},{4,5},{5,4},{6,7},{7,6},{8,9},{9,8},{10,11... | collective-permute-start | bytes 3145736 | tf_op jit(solution)/shard_map/ppermute | solution.py:53
  55.3 42.7 %copy-start.4 = (bf16[1024,1024]{1,0:T(8,128)(2,1)S(1)}, bf16[1024,1024]{1,0:T(8,128)(2,1)}, u32[]{:S(2)}) copy-start(bf16[1024,1024]{1,0:T(8,128)(2,1)} %fusion.2.pick_ref) | copy-start | bytes 6291460
  55.3 37.9 %collective-permute-start.5 = (bf16[128,4096]{1,0:T(8,128)(2,1)S(1)}, bf16[128,4096]{1,0:T(8,128)(2,1)S(1)}, u32[]{:S(2)}, u32[]{:S(2)}) collective-permute-start(bf16[128,4096]{1,0:T(8,128)(2,1)S(1)} %add_convert_fusion.1.near_ref), channel_id=1, source_target_pairs={{0,2},{2,0},{1,3},{3,1},{4,6},{6,4},{5,7},{7,5},{8,10},{10,8},{9,1... | collective-permute-start | bytes 3145736 | tf_op jit(solution)/shard_map/ppermute | solution.py:57
  57.4 15.1 %collective-permute-start.9 = (bf16[272,512]{1,0:T(8,128)(2,1)S(1)}, bf16[272,512]{1,0:T(8,128)(2,1)S(1)}, u32[]{:S(2)}, u32[]{:S(2)}) collective-permute-start(bf16[272,512]{1,0:T(8,128)(2,1)S(1)} %get-tuple-element.53.q_pack.refs_0_), channel_id=1, source_target_pairs={{8,0},{12,4},{16,8},{20,12},{24,16},{28,20},{32,24},{36,28},{40,32... | collective-permute-start | bytes 835592 | tf_op jit(solution)/shard_map/ppermute | solution.py:66
  59.3 18.2 %collective-permute-start.8 = (bf16[272,512]{1,0:T(8,128)(2,1)S(1)}, bf16[272,512]{1,0:T(8,128)(2,1)S(1)}, u32[]{:S(2)}, u32[]{:S(2)}) collective-permute-start(bf16[272,512]{1,0:T(8,128)(2,1)S(1)} %get-tuple-element.53.q_pack.refs_0_), channel_id=1, source_target_pairs={{4,0},{8,4},{12,8},{16,12},{20,16},{24,20},{28,24},{32,28},{36,32}... | collective-permute-start | bytes 835592 | tf_op jit(solution)/shard_map/ppermute | solution.py:66
  61.3 16.2 %collective-permute-start.7 = (bf16[272,512]{1,0:T(8,128)(2,1)S(1)}, bf16[272,512]{1,0:T(8,128)(2,1)S(1)}, u32[]{:S(2)}, u32[]{:S(2)}) collective-permute-start(bf16[272,512]{1,0:T(8,128)(2,1)S(1)} %get-tuple-element.53.q_pack.refs_0_), channel_id=1, source_target_pairs={{0,4},{4,8},{8,12},{12,16},{16,20},{20,24},{24,28},{28,32},{32,36}... | collective-permute-start | bytes 835592 | tf_op jit(solution)/shard_map/ppermute | solution.py:66
  67.6 14.5 %collective-permute-start.6 = (bf16[272,512]{1,0:T(8,128)(2,1)S(1)}, bf16[272,512]{1,0:T(8,128)(2,1)S(1)}, u32[]{:S(2)}, u32[]{:S(2)}) collective-permute-start(bf16[272,512]{1,0:T(8,128)(2,1)S(1)} %get-tuple-element.53.q_pack.refs_0_), channel_id=1, source_target_pairs={{0,8},{4,12},{8,16},{12,20},{16,24},{20,28},{24,32},{28,36},{32,40... | collective-permute-start | bytes 835592 | tf_op jit(solution)/shard_map/ppermute | solution.py:66
  72.5 30.3 %copy-start.22 = (bf16[272,512]{1,0:T(8,128)(2,1)}, bf16[272,512]{1,0:T(8,128)(2,1)S(1)}, u32[]{:S(2)}) copy-start(bf16[272,512]{1,0:T(8,128)(2,1)S(1)} %collective-permute-done.9.refs_2_) | copy-start | bytes 835588
  77.5 25.3 %copy-start.18 = (bf16[272,512]{1,0:T(8,128)(2,1)}, bf16[272,512]{1,0:T(8,128)(2,1)S(1)}, u32[]{:S(2)}) copy-start(bf16[272,512]{1,0:T(8,128)(2,1)S(1)} %collective-permute-done.8.refs_4_) | copy-start | bytes 835588
  77.5 25.3 %copy-start.20 = (bf16[272,512]{1,0:T(8,128)(2,1)}, bf16[272,512]{1,0:T(8,128)(2,1)S(1)}, u32[]{:S(2)}) copy-start(bf16[272,512]{1,0:T(8,128)(2,1)S(1)} %collective-permute-done.7.refs_2_) | copy-start | bytes 835588
  82.2 20.6 %copy-start.24 = (bf16[272,512]{1,0:T(8,128)(2,1)}, bf16[272,512]{1,0:T(8,128)(2,1)S(1)}, u32[]{:S(2)}) copy-start(bf16[272,512]{1,0:T(8,128)(2,1)S(1)} %collective-permute-done.6.refs_0_) | copy-start | bytes 835588
  93.2 12.5 %slice-start.2 = ((s8[8388608]{0:T(1024)(128)(4,1)}), s8[4194304]{0:T(1024)(128)(4,1)S(1)}, s32[]{:S(2)}) async-start(s8[8388608]{0:T(1024)(128)(4,1)} %bitcast.41), calls=%async_computation.2 | async-start | bytes 8388608
  94.4 8.4 %copy-start.7 = (f32[128,4096]{1,0:T(8,128)}, f32[128,4096]{1,0:T(8,128)S(1)}, u32[]{:S(2)}) copy-start(f32[128,4096]{1,0:T(8,128)S(1)} %get-tuple-element.56.unit_ref) | copy-start | bytes 6291460
  94.4 3.6 %collective-permute-start.10 = (bf16[128,4096]{1,0:T(8,128)(2,1)S(1)}, bf16[128,4096]{1,0:T(8,128)(2,1)S(1)}, u32[]{:S(2)}, u32[]{:S(2)}) collective-permute-start(bf16[128,4096]{1,0:T(8,128)(2,1)S(1)} %get-tuple-element.57.own_ref), channel_id=1, source_target_pairs={{0,1},{1,0},{2,3},{3,2},{4,5},{5,4},{6,7},{7,6},{8,9},{9,8},{10,11... | collective-permute-start | bytes 3145736 | tf_op jit(solution)/shard_map/ppermute | solution.py:53
  98.0 7.7 %slice-start.3 = ((s8[8388608]{0:T(1024)(128)(4,1)}), s8[4194304]{0:T(1024)(128)(4,1)S(1)}, s32[]{:S(2)}) async-start(s8[8388608]{0:T(1024)(128)(4,1)} %bitcast.41), calls=%async_computation.3 | async-start | bytes 8388608
  105.2 2.9 %collective-permute-start.11 = (bf16[128,4096]{1,0:T(8,128)(2,1)S(1)}, bf16[128,4096]{1,0:T(8,128)(2,1)S(1)}, u32[]{:S(2)}, u32[]{:S(2)}) collective-permute-start(bf16[128,4096]{1,0:T(8,128)(2,1)S(1)} %get-tuple-element.63), channel_id=1, source_target_pairs={{0,1},{1,0},{2,3},{3,2},{4,5},{5,4},{6,7},{7,6},{8,9},{9,8},{10,11... | collective-permute-start | bytes 3145736 | tf_op jit(solution)/shard_map/ppermute | solution.py:53
  110.4 4.1 %collective-permute-start.13 = (bf16[128,4096]{1,0:T(8,128)(2,1)S(1)}, bf16[128,4096]{1,0:T(8,128)(2,1)}, u32[]{:S(2)}, u32[]{:S(2)}) collective-permute-start(bf16[128,4096]{1,0:T(8,128)(2,1)S(1)} %slice.17), channel_id=1, source_target_pairs={{0,1},{1,0},{2,3},{3,2},{4,5},{5,4},{6,7},{7,6},{8,9},{9,8},{10,11... | collective-permute-start | bytes 3145736 | tf_op jit(solution)/shard_map/ppermute | solution.py:53
  110.6 4.0 %copy-start.33 = (bf16[256,4096]{1,0:T(8,128)(2,1)S(1)}, bf16[256,4096]{1,0:T(8,128)(2,1)}, u32[]{:S(2)}) copy-start(bf16[256,4096]{1,0:T(8,128)(2,1)} %copy-done.32) | copy-start | bytes 6291460
  112.2 26.2 %collective-permute-start.12 = (bf16[128,4096]{1,0:T(8,128)(2,1)S(1)}, bf16[128,4096]{1,0:T(8,128)(2,1)S(1)}, u32[]{:S(2)}, u32[]{:S(2)}) collective-permute-start(bf16[128,4096]{1,0:T(8,128)(2,1)S(1)} %add_convert_fusion.near_ref), channel_id=1, source_target_pairs={{0,2},{2,0},{1,3},{3,1},{4,6},{6,4},{5,7},{7,5},{8,10},{10,8},{9,1... | collective-permute-start | bytes 3145736 | tf_op jit(solution)/shard_map/ppermute | solution.py:57
  116.0 22.4 %copy-start.8 = (f32[128,4096]{1,0:T(8,128)S(1)}, f32[128,4096]{1,0:T(8,128)}, u32[]{:S(2)}) copy-start(f32[128,4096]{1,0:T(8,128)} %copy-done.7) | copy-start | bytes 6291460
  116.0 22.4 %copy-start.11 = (bf16[2,1,64,4096]{3,2,1,0:T(8,128)(2,1)S(1)}, bf16[2,1,64,4096]{3,2,1,0:T(8,128)(2,1)}, u32[]{:S(2)}) copy-start(bf16[2,1,64,4096]{3,2,1,0:T(8,128)(2,1)} %copy-done.10) | copy-start | bytes 3145732
  139.7 3.6 %collective-permute-start.14 = (bf16[128,4096]{1,0:T(8,128)(2,1)S(1)}, bf16[128,4096]{1,0:T(8,128)(2,1)S(1)}, u32[]{:S(2)}, u32[]{:S(2)}) collective-permute-start(bf16[128,4096]{1,0:T(8,128)(2,1)S(1)} %shard_map.151.own_ref), channel_id=1, source_target_pairs={{0,1},{1,0},{2,3},{3,2},{4,5},{5,4},{6,7},{7,6},{8,9},{9,8},{10,11... | collective-permute-start | bytes 3145736 | tf_op jit(solution)/shard_map/ppermute | solution.py:53
  143.3 2.2 %copy-start.3 = (bf16[512,4096]{1,0:T(8,128)(2,1)S(1)}, bf16[512,4096]{1,0:T(8,128)(2,1)}, u32[]{:S(2)}) copy-start(bf16[512,4096]{1,0:T(8,128)(2,1)} %weight_ref.3) | copy-start | bytes 12582916
  146.4 18.4 %copy-start.35 = (bf16[64,4096]{1,0:T(8,128)(2,1)S(1)}, bf16[64,4096]{1,0:T(8,128)(2,1)}, u32[]{:S(2)}) copy-start(bf16[64,4096]{1,0:T(8,128)(2,1)} %select_convert_fusion) | copy-start | bytes 1572868
  147.9 27.1 %collective-permute-start.19 = (bf16[272,512]{1,0:T(8,128)(2,1)S(1)}, bf16[272,512]{1,0:T(8,128)(2,1)S(1)}, u32[]{:S(2)}, u32[]{:S(2)}) collective-permute-start(bf16[272,512]{1,0:T(8,128)(2,1)S(1)} %get-tuple-element.71.do_pack.refs_1_), channel_id=1, source_target_pairs={{4,0},{8,4},{12,8},{16,12},{20,16},{24,20},{28,24},{32,28},{36,32}... | collective-permute-start | bytes 835592 | tf_op jit(solution)/shard_map/ppermute | solution.py:66
  149.8 25.2 %collective-permute-start.18 = (bf16[272,512]{1,0:T(8,128)(2,1)S(1)}, bf16[272,512]{1,0:T(8,128)(2,1)S(1)}, u32[]{:S(2)}, u32[]{:S(2)}) collective-permute-start(bf16[272,512]{1,0:T(8,128)(2,1)S(1)} %get-tuple-element.71.do_pack.refs_1_), channel_id=1, source_target_pairs={{0,4},{4,8},{8,12},{12,16},{16,20},{20,24},{24,28},{28,32},{32,36}... | collective-permute-start | bytes 835592 | tf_op jit(solution)/shard_map/ppermute | solution.py:66
  156.2 21.5 %collective-permute-start.17 = (bf16[272,512]{1,0:T(8,128)(2,1)S(1)}, bf16[272,512]{1,0:T(8,128)(2,1)S(1)}, u32[]{:S(2)}, u32[]{:S(2)}) collective-permute-start(bf16[272,512]{1,0:T(8,128)(2,1)S(1)} %get-tuple-element.71.do_pack.refs_1_), channel_id=1, source_target_pairs={{8,0},{12,4},{16,8},{20,12},{24,16},{28,20},{32,24},{36,28},{40,32... | collective-permute-start | bytes 835592 | tf_op jit(solution)/shard_map/ppermute | solution.py:66
  158.7 18.9 %collective-permute-start.16 = (bf16[272,512]{1,0:T(8,128)(2,1)S(1)}, bf16[272,512]{1,0:T(8,128)(2,1)S(1)}, u32[]{:S(2)}, u32[]{:S(2)}) collective-permute-start(bf16[272,512]{1,0:T(8,128)(2,1)S(1)} %get-tuple-element.71.do_pack.refs_1_), channel_id=1, source_target_pairs={{0,8},{4,12},{8,16},{12,20},{16,24},{20,28},{24,32},{28,36},{32,40... | collective-permute-start | bytes 835592 | tf_op jit(solution)/shard_map/ppermute | solution.py:66
  164.8 21.5 %collective-permute-start.15 = (bf16[64,4096]{1,0:T(8,128)(2,1)S(1)}, bf16[64,4096]{1,0:T(8,128)(2,1)S(1)}, u32[]{:S(2)}, u32[]{:S(2)}) collective-permute-start(bf16[64,4096]{1,0:T(8,128)(2,1)S(1)} %copy-done.35), channel_id=1, source_target_pairs={{0,2},{2,0},{1,3},{3,1},{4,6},{6,4},{5,7},{7,5},{8,10},{10,8},{9,1... | collective-permute-start | bytes 1572872 | tf_op jit(solution)/shard_map/ppermute | solution.py:57
  173.9 3.8 %copy-start.23 = (bf16[272,512]{1,0:T(8,128)(2,1)S(1)}, bf16[272,512]{1,0:T(8,128)(2,1)}, u32[]{:S(2)}) copy-start(bf16[272,512]{1,0:T(8,128)(2,1)} %copy-done.22) | copy-start | bytes 835588
  173.9 3.8 %copy-start.25 = (bf16[272,512]{1,0:T(8,128)(2,1)S(1)}, bf16[272,512]{1,0:T(8,128)(2,1)}, u32[]{:S(2)}) copy-start(bf16[272,512]{1,0:T(8,128)(2,1)} %copy-done.24) | copy-start | bytes 835588
  175.0 11.3 %copy-start.9 = (f32[128,4096]{1,0:T(8,128)S(1)}, f32[128,4096]{1,0:T(8,128)}, u32[]{:S(2)}) copy-start(f32[128,4096]{1,0:T(8,128)} %copy-done.7) | copy-start | bytes 6291460
  175.0 11.3 %copy-start.31 = (f32[64,4096]{1,0:T(8,128)S(1)}, f32[64,4096]{1,0:T(8,128)}, u32[]{:S(2)}) copy-start(f32[64,4096]{1,0:T(8,128)} %slice_select_fusion) | copy-start | bytes 3145732
  177.7 9.7 %copy-start.1 = (bf16[256,4096]{1,0:T(8,128)(2,1)S(1)}, bf16[256,4096]{1,0:T(8,128)(2,1)}, u32[]{:S(2)}) copy-start(bf16[256,4096]{1,0:T(8,128)(2,1)} %param.14) | copy-start | bytes 6291460
  (12 other events, 14.1 us)
where the time goes:
time: 188 us; the launch traced here: 187 us
  waiting for transfers between devices  66.6 us (35%)
  starting transfers between devices  60 us (32%)
  Pallas kernels  26.8 us (14%)
  other arithmetic  12.8 us (7%)
  matrix products  10.7 us (6%)
  local copies, waits for them, and re-layouts  9.33 us (5%)
    ppermute x12, starting transfers between devices, from_behind(): lax.ppermute(array, 'seq', [(i, i + by) for i in range(count) if 0 <= i +...  47.1 us
    ppermute x3, waiting for transfers between devices, swap_chip(): return lax.ppermute(array, 'tp', [(0, 2), (2, 0), (1, 3), (3, 1)])  37.2 us
    ppermute x12, waiting for transfers between devices, from_behind(): lax.ppermute(array, 'seq', [(i, i + by) for i in range(count) if 0 <= i +...  22.6 us
    unnamed x80, local copies, waits for them, and re-layouts  7.28 us
    ppermute x5, waiting for transfers between devices, swap_core(): return lax.ppermute(array, 'tp', [(0, 1), (1, 0), (2, 3), (3, 2)])  6.87 us
    ppermute x3, starting transfers between devices, swap_chip(): return lax.ppermute(array, 'tp', [(0, 2), (2, 0), (1, 3), (3, 1)])  6.52 us
    ppermute x5, starting transfers between devices, swap_core(): return lax.ppermute(array, 'tp', [(0, 1), (1, 0), (2, 3), (3, 2)])  6.31 us
    dot_general x1, matrix products, dot_nt(): return lax.dot_general(a, b, NT, preferred_element_type=F32)  6.12 us
  transfers between devices with their start and end apart: 20, of which 11 were waited for; matrix products, arithmetic and copies ran while one was open for 12% of the time, Pallas kernels for 6%

commit v1 on v0

--- a/solution.py
+++ b/solution.py
@@ -61,9 +61,15 @@
     return lax.optimization_barrier((value, earlier))[0]
 
 
-def from_behind(array, by):
+def swap_block(array, first):
     count = lax.axis_size("seq")
-    return lax.ppermute(array, "seq", [(i, i + by) for i in range(count) if 0 <= i + by < count])
+    ahead = [(i, i + 1) for i in range(first, count - 1, 2)]
+    return lax.ppermute(array, "seq", ahead + [(j, i) for i, j in ahead])
+
+
+def nearby_offsets(seq):
+    side = 1 - 2 * (seq % 2)
+    return side, -side, 2 * side, -2 * side
 
 
 def three_parts(values):
@@ -107,7 +113,7 @@
         query = pack_ref[:rows, cols]
         scores = []
         values = []
-        for offset, pair in ((0, None), (-2, kv_a), (-1, kv_b), (1, kv_c), (2, kv_d)):
+        for offset, pair in zip((0,) + nearby_offsets(seq), (None, kv_a, kv_b, kv_c, kv_d)):
             key = k0[:, cols] if pair is None else pair[0, :, cols]
             values.append(v0[:, cols] if pair is None else pair[1, :, cols])
             score = dot_nt(query, key) * (scale * LOG2E)
@@ -250,7 +256,7 @@
         query, out_grad = q_pack[:rows, cols], do_pack[:rows, cols]
         lse, delta = lse_ref[:, head : head + 1], delta_ref[:, head : head + 1]
         total = jnp.zeros((rows, HEAD_DIM), F32)
-        for offset, pair in ((0, None), (-2, kv_a), (-1, kv_b), (1, kv_c), (2, kv_d)):
+        for offset, pair in zip((0,) + nearby_offsets(seq), (None, kv_a, kv_b, kv_c, kv_d)):
             key = k0[:, cols] if pair is None else pair[0, :, cols]
             value = v0[:, cols] if pair is None else pair[1, :, cols]
             score = dot_nt(query, key) * (scale * LOG2E) - lse
@@ -316,8 +322,7 @@
     place = jnp.stack([seq, jnp.full_like(seq, blocks), core]).astype(jnp.int32)
 
     kv = jnp.stack([key_heads, value_heads])
-    behind1 = from_behind(kv, 1)
-    ahead1 = from_behind(kv, -1)
+    kv_a, kv_b = swap_block(kv, 0), swap_block(kv, 1)
 
     def half_rows(array, place):
         split = array.reshape(2, 2, half // 2, array.shape[1])
@@ -326,9 +331,8 @@
     cot_own = half_rows(cotangent, core)
     cot_local = jnp.concatenate([cot_own, half_rows(cotangent, 1 - core)], axis=0)
     grad_merged = dot_nt(cot_local, down_source)
-    behind1, ahead1, grad_merged = lax.optimization_barrier((behind1, ahead1, grad_merged))
-    behind2 = from_behind(behind1, 1)
-    ahead2 = from_behind(ahead1, -1)
+    kv_a, kv_b, grad_merged = lax.optimization_barrier((kv_a, kv_b, grad_merged))
+    kv_c, kv_d = swap_block(kv_b, 0), swap_block(kv_a, 1)
 
     residual_own = half_rows(residual, core)
     local_source = neuron_source - tp_place * src_width
@@ -343,10 +347,10 @@
     gain_row = ln_gain.reshape(1, model_width)
     inverse_row = inverse.reshape(1, src_width)
     copy_row = copy_gain.reshape(1, src_width)
-    behind2, ahead2, pick, grad_merged, grad_copy, residual_own = lax.optimization_barrier(
-        (behind2, ahead2, pick, grad_merged, grad_copy, residual_own)
+    kv_c, kv_d, pick, grad_merged, grad_copy, residual_own = lax.optimization_barrier(
+        (kv_c, kv_d, pick, grad_merged, grad_copy, residual_own)
     )
-    window = (key_heads, value_heads, behind2, behind1, ahead1, ahead2)
+    window = (key_heads, value_heads, kv_a, kv_b, kv_c, kv_d)
 
     attended, q_pack, lse = call(
         functools.partial(attention_kernel, scale),
@@ -358,17 +362,15 @@
         [SMEM] + [VMEM] * 7,
     )(place, query_heads, *window)
 
-    def chip_sum(kernel, operands, beside):
+    def chip_sum(kernel, operands):
         own, other = call(kernel, (shape((half, model_width), BF16),) * 2, [VMEM, VMEM])(*operands)
-        other, beside = lax.optimization_barrier((swap_core(other), beside))
-        near = (own.astype(F32) + other.astype(F32)).astype(BF16)
-        return near, swap_chip(near), beside
-
-    near, far, _ = chip_sum(out_kernel, (attended, out_weight), ())
+        near = (own.astype(F32) + swap_core(other).astype(F32)).astype(BF16)
+        return near, swap_chip(near)
+
+    near, far = chip_sum(out_kernel, (attended, out_weight))
 
     q_early = after(q_pack, near)
-    q_packs = {offset: from_behind(q_early, -offset) for offset in (-1, 1, -2, 2)}
-    far, q_packs = lax.optimization_barrier((far, q_packs))
+    far, q_a, q_b = lax.optimization_barrier((far, swap_block(q_early, 0), swap_block(q_early, 1)))
 
     unit, sigma, normed = call(
         norm_kernel,
@@ -383,13 +385,11 @@
     merged, hidden_grad = call(ffn_kernel, (shape((rows, src_width), BF16),) * 2, [VMEM] * 8)(
         normed, near_normed, up_source, pick, grad_merged, grad_copy, inverse_row, copy_row
     )
+    near, far = chip_sum(back_kernel, (hidden_grad, up_source))
     ffn_part = dot(merged, down_source).astype(BF16)
-    near, far, ffn_part = chip_sum(back_kernel, (hidden_grad, up_source), ffn_part)
-    ffn_near = swap_core(ffn_part[half:])
-    ffn_chip = (ffn_part[:half].astype(F32) + ffn_near.astype(F32)).reshape(2, half // 2, model_width)
-    ffn_send = jnp.where(chip == 0, ffn_chip[1], ffn_chip[0]).astype(BF16)
-    ffn_mine = jnp.where(chip == 0, ffn_chip[0], ffn_chip[1])
-    far, ffn_send, ffn_mine = lax.optimization_barrier((far, ffn_send, ffn_mine))
+    q_c, q_d = after((q_b, q_a), near)
+    q_c, q_d = swap_block(q_c, 0), swap_block(q_d, 1)
+    far, ffn_part, q_c, q_d = lax.optimization_barrier((far, ffn_part, q_c, q_d))
 
     low = call(
         norm_back_kernel,
@@ -397,22 +397,28 @@
         [VMEM] * 6,
         scratch=[pltpu.VMEM((half, model_width), F32)],
     )(near, far, cot_own, gain_row, unit, sigma)
-    near_low = swap_core(low)
+    ffn_part = after(ffn_part, low)
+    near_low, ffn_near = lax.optimization_barrier((swap_core(low), swap_core(ffn_part[half:])))
     do_pack, delta = call(
         grad_attended_kernel,
         (shape((rows + STAT_ROWS, head_width), BF16), shape((rows, HEAD_DIM), F32)),
         [VMEM] * 4,
     )(low, near_low, out_weight, attended)
 
-    do_packs = {offset: from_behind(do_pack, -offset) for offset in (-2, 2, -1, 1)}
-
-    ffn_far = swap_chip(after(ffn_send, do_pack))
-
+    do_a, do_b = swap_block(do_pack, 0), swap_block(do_pack, 1)
+
+    ffn_part = after(ffn_part, do_pack)
+    ffn_chip = (ffn_part[:half].astype(F32) + ffn_near.astype(F32)).reshape(2, half // 2, model_width)
+    ffn_far = swap_chip(jnp.where(chip == 0, ffn_chip[1], ffn_chip[0]).astype(BF16))
+    ffn_mine = jnp.where(chip == 0, ffn_chip[0], ffn_chip[1])
+
+    do_a, do_b, do_own = lax.optimization_barrier((do_a, do_b, do_pack))
+    do_c, do_d = swap_block(do_b, 0), swap_block(do_a, 1)
     grad_query = call(
         functools.partial(grad_query_kernel, scale),
         shape((rows, head_width), F32),
         [SMEM] + [VMEM] * 10,
-    )(place, q_pack, do_pack, lse, delta, *window)
+    )(place, q_pack, do_own, lse, delta, *window)
 
     def grad_key_value(pairs, sums):
         return call(
@@ -421,13 +427,10 @@
             [VMEM] * (2 * len(pairs) + 2 + len(sums)),
         )(*[pack for pair in pairs for pack in pair], key_heads, value_heads, *sums)
 
-    sums = grad_key_value(
-        [(q_pack, do_pack)] + [(q_packs[offset], do_packs[offset]) for offset in (-1, 1)], ()
-    )
+    sums = grad_key_value([(q_pack, do_own), (q_a, do_a), (q_b, do_b)], ())
     own_unit = lax.dynamic_slice_in_dim(unit, chip * (half // 2), half // 2, 0)
     encoded = own_unit * ln_gain + (ffn_mine + ffn_far.astype(F32))
-    far_pairs = [(q_packs[offset], do_packs[offset]) for offset in (-2, 2)]
-    grad_key, grad_value = grad_key_value(far_pairs, sums)
+    grad_key, grad_value = grad_key_value([(q_c, do_c), (q_d, do_d)], sums)
 
     col_width = model_width // lax.axis_size("tp")
     first = jnp.where(core == 0, low, near_low).reshape(2, half // 2, model_width)

time: 188 us -> 178 us (0.947)
  the two profiles are of different devices: /device:TPU:109 before, /device:TPU:5 now
where the time goes in v1:
time: 178 us; the launch traced here: 177 us
  waiting for transfers between devices  76.9 us (43%)
  starting transfers between devices  45.1 us (25%)
  Pallas kernels  27.5 us (15%)
  matrix products  10.3 us (6%)
  other arithmetic  9.55 us (5%)
  local copies, waits for them, and re-layouts  6.34 us (4%)
    ppermute x3, waiting for transfers between devices, swap_chip(): return lax.ppermute(array, 'tp', [(0, 2), (2, 0), (1, 3), (3, 1)])  40.1 us
    ppermute x12, starting transfers between devices, swap_block(): return lax.ppermute(array, 'seq', ahead + [(j, i) for i, j in ahead])  31.2 us
    ppermute x12, waiting for transfers between devices, swap_block(): return lax.ppermute(array, 'seq', ahead + [(j, i) for i, j in ahead])  25.9 us
    ppermute x5, waiting for transfers between devices, swap_core(): return lax.ppermute(array, 'tp', [(0, 1), (1, 0), (2, 3), (3, 2)])  11 us
    ppermute x3, starting transfers between devices, swap_chip(): return lax.ppermute(array, 'tp', [(0, 2), (2, 0), (1, 3), (3, 1)])  8.11 us
    ppermute x5, starting transfers between devices, swap_core(): return lax.ppermute(array, 'tp', [(0, 1), (1, 0), (2, 3), (3, 2)])  5.8 us
    dot_general x1, matrix products, dot_nt(): return lax.dot_general(a, b, NT, preferred_element_type=F32)  5.74 us
    pallas_call x1, Pallas kernels, shards(): call(functools.partial(grad_query_kernel, scale), shape((rows, head_width...  5.56 us
  transfers between devices with their start and end apart: 20, of which 14 were waited for; matrix products, arithmetic and copies ran while one was open for 11% of the time, Pallas kernels for 5%

profile of v1, /device:TPU:5, one launch (start us, length us, event | category | flops | bytes accessed | tf_op | source)
XLA Modules:
  0.0 177.0 jit_solution(5097902712784938375)
XLA Ops:
  0.6 1.2 pad_maximum_fusion.1
  1.9 6.7 %collective-permute-start.1 = (bf16[2,256,512]{2,1,0:T(8,128)(2,1)S(1)}, bf16[2,256,512]{2,1,0:T(8,128)(2,1)S(1)}, u32[]{:S(2)}, u32[]{:S(2)}) collective-permute-start(bf16[2,256,512]{2,1,0:T(8,128)(2,1)S(1)} %pad_maximum_fusion.1), channel_id=1, source_target_pairs={{4,8},{12,16},{20,24},{28,32},{36,40},{44,48},{52,56},{60,64},{68,... | collective-permute-start | bytes 1572872 | tf_op jit(solution)/shard_map/ppermute | solution.py:67
  8.6 0.7 broadcast_subtract_fusion
  9.8 2.2 %fusion.2.pick_ref = bf16[1024,1024]{1,0:T(8,128)(2,1)} fusion(s32[1024]{0:T(1024)S(1)} %broadcast_subtract_fusion), kind=kLoop, calls=%fused_computation.5 | loop fusion | flops 2097152 | bytes 2101248 | tf_op jit(solution)/shard_map/convert_element_type | solution.py:341
  12.1 1.7 constant_dynamic-slice_fusion.2
  13.8 5.7 %fusion.3 = f32[256,1024]{1,0:T(8,128)S(1)} fusion(bf16[1024,4096]{1,0:T(8,128)(2,1)} %param.18, bf16[128,4096]{1,0:T(8,128)(2,1)S(1)} %bitcast.40, bf16[128,4096]{1,0:T(8,128)(2,1)S(1)} %bitcast.29), kind=kOutput, calls=%fused_computation.6 | convolution fusion | flops 2151677952 | bytes 11534336 | tf_op jit(solution)/shard_map/dot_general | solution.py:49
  20.2 1.0 collective-permute-done.kv_a
  21.2 5.0 %collective-permute-start.3 = (bf16[2,256,512]{2,1,0:T(8,128)(2,1)}, bf16[2,256,512]{2,1,0:T(8,128)(2,1)S(1)}, u32[]{:S(2)}, u32[]{:S(2)}) collective-permute-start(bf16[2,256,512]{2,1,0:T(8,128)(2,1)} %collective-permute-done.kv_a), channel_id=1, source_target_pairs={{4,8},{12,16},{20,24},{28,32},{36,40},{44,48},{52,56},{60,64},{68,... | collective-permute-start | bytes 1572872 | tf_op jit(solution)/shard_map/ppermute | solution.py:67
  26.5 1.1 fusion
  27.6 1.0 fusion.10.grad_copy_ref
  28.7 9.2 %collective-permute-done.3.kv_d = bf16[2,256,512]{2,1,0:T(8,128)(2,1)S(1)} collective-permute-done((bf16[2,256,512]{2,1,0:T(8,128)(2,1)}, bf16[2,256,512]{2,1,0:T(8,128)(2,1)S(1)}, u32[]{:S(2)}, u32[]{:S(2)}) %collective-permute-start.3) | collective-permute-done | bytes 524320 | tf_op jit(solution)/shard_map/ppermute | solution.py:67
  37.9 3.9 %shard_map.146 = (bf16[256,512]{1,0:T(8,128)(2,1)S(1)}, bf16[272,512]{1,0:T(8,128)(2,1)S(1)}, f32[256,128]{1,0:T(8,128)S(1)}) custom-call(s32[3]{0:T(128)S(1)} %pad_add_fusion.place, bf16[256,512]{1,0:T(8,128)(2,1)S(1)} %copy-done.23, bf16[256,512]{1,0:T(8,128)(2,1)S(1)} %copy-done.5, bf16[256,512]{1,0:T(8,128)(2,1)S(1)} %copy-done.6, ...), custom_call_target="tpu_custom_call" | custom-call | flops 1024 | bytes 1024 | tf_op jit(solution)/shard_map/pallas_call | solution.py:355
  41.9 1.3 shard_map.147
  43.2 2.9 %collective-permute-start.4 = (bf16[128,4096]{1,0:T(8,128)(2,1)S(1)}, bf16[128,4096]{1,0:T(8,128)(2,1)S(1)}, u32[]{:S(2)}, u32[]{:S(2)}) collective-permute-start(bf16[128,4096]{1,0:T(8,128)(2,1)S(1)} %get-tuple-element.56), channel_id=1, source_target_pairs={{0,1},{1,0},{2,3},{3,2},{4,5},{5,4},{6,7},{7,6},{8,9},{9,8},{10,11... | collective-permute-start | bytes 3145736 | tf_op jit(solution)/shard_map/ppermute | solution.py:53
  46.1 2.3 %collective-permute-done.4 = bf16[128,4096]{1,0:T(8,128)(2,1)S(1)} collective-permute-done((bf16[128,4096]{1,0:T(8,128)(2,1)S(1)}, bf16[128,4096]{1,0:T(8,128)(2,1)S(1)}, u32[]{:S(2)}, u32[]{:S(2)}) %collective-permute-start.4) | collective-permute-done | bytes 1048608 | tf_op jit(solution)/shard_map/ppermute | solution.py:53
  48.7 2.7 %collective-permute-start.5 = (bf16[128,4096]{1,0:T(8,128)(2,1)S(1)}, bf16[128,4096]{1,0:T(8,128)(2,1)S(1)}, u32[]{:S(2)}, u32[]{:S(2)}) collective-permute-start(bf16[128,4096]{1,0:T(8,128)(2,1)S(1)} %add_convert_fusion.1.near_ref), channel_id=1, source_target_pairs={{0,2},{2,0},{1,3},{3,1},{4,6},{6,4},{5,7},{7,5},{8,10},{10,8},{9,1... | collective-permute-start | bytes 3145736 | tf_op jit(solution)/shard_map/ppermute | solution.py:57
  51.4 4.4 %collective-permute-start.7 = (bf16[272,512]{1,0:T(8,128)(2,1)S(1)}, bf16[272,512]{1,0:T(8,128)(2,1)S(1)}, u32[]{:S(2)}, u32[]{:S(2)}) collective-permute-start(bf16[272,512]{1,0:T(8,128)(2,1)S(1)} %get-tuple-element.58.q_pack.refs_0_), channel_id=1, source_target_pairs={{4,8},{12,16},{20,24},{28,32},{36,40},{44,48},{52,56},{60,64},{68,... | collective-permute-start | bytes 835592 | tf_op jit(solution)/shard_map/ppermute | solution.py:67
  56.1 7.8 %collective-permute-done.7.refs_4_ = bf16[272,512]{1,0:T(8,128)(2,1)S(1)} collective-permute-done((bf16[272,512]{1,0:T(8,128)(2,1)S(1)}, bf16[272,512]{1,0:T(8,128)(2,1)S(1)}, u32[]{:S(2)}, u32[]{:S(2)}) %collective-permute-start.7) | collective-permute-done | bytes 278560 | tf_op jit(solution)/shard_map/ppermute | solution.py:67
  63.9 16.7 %collective-permute-done.5.far_ref = bf16[128,4096]{1,0:T(8,128)(2,1)S(1)} collective-permute-done((bf16[128,4096]{1,0:T(8,128)(2,1)S(1)}, bf16[128,4096]{1,0:T(8,128)(2,1)S(1)}, u32[]{:S(2)}, u32[]{:S(2)}) %collective-permute-start.5) | collective-permute-done | bytes 1048608 | tf_op jit(solution)/shard_map/ppermute | solution.py:57
  80.6 1.2 shard_map.148
  81.8 1.3 collective-permute-start.8
  83.1 2.3 %collective-permute-done.8.near_ref = bf16[128,4096]{1,0:T(8,128)(2,1)S(1)} collective-permute-done((bf16[128,4096]{1,0:T(8,128)(2,1)S(1)}, bf16[128,4096]{1,0:T(8,128)(2,1)S(1)}, u32[]{:S(2)}, u32[]{:S(2)}) %collective-permute-start.8) | collective-permute-done | bytes 1048608 | tf_op jit(solution)/shard_map/ppermute | solution.py:53
  85.4 4.8 %shard_map.149 = (bf16[256,1024]{1,0:T(8,128)(2,1)S(1)}, bf16[256,1024]{1,0:T(8,128)(2,1)S(1)}) custom-call(bf16[128,4096]{1,0:T(8,128)(2,1)S(1)} %get-tuple-element.62.own_ref, bf16[128,4096]{1,0:T(8,128)(2,1)S(1)} %collective-permute-done.8.near_ref, bf16[4096,1024]{1,0:T(8,128)(2,1)S(1)} %bitcast.26, bf16[1024,1024]{1,0:T(8,128)(2,1)S(1)} %copy-done.4, ...), custom_call_target="tpu_custom_call" | custom-call | flops 1024 | bytes 1024 | tf_op jit(solution)/shard_map/pallas_call | solution.py:385
  90.2 2.4 %shard_map.150 = (bf16[128,4096]{1,0:T(8,128)(2,1)S(1)}, bf16[128,4096]{1,0:T(8,128)(2,1)S(1)}) custom-call(bf16[256,1024]{1,0:T(8,128)(2,1)S(1)} %get-tuple-element.66.hidden_grad_ref, bf16[4096,1024]{1,0:T(8,128)(2,1)S(1)} %bitcast.26), custom_call_target="tpu_custom_call" | custom-call | flops 1024 | bytes 1024 | tf_op jit(solution)/shard_map/pallas_call | solution.py:366
  93.0 2.3 %collective-permute-done.9 = bf16[128,4096]{1,0:T(8,128)(2,1)S(1)} collective-permute-done((bf16[128,4096]{1,0:T(8,128)(2,1)S(1)}, bf16[128,4096]{1,0:T(8,128)(2,1)S(1)}, u32[]{:S(2)}, u32[]{:S(2)}) %collective-permute-start.9) | collective-permute-done | bytes 1048608 | tf_op jit(solution)/shard_map/ppermute | solution.py:53
  95.6 2.7 %collective-permute-start.10 = (bf16[128,4096]{1,0:T(8,128)(2,1)S(1)}, bf16[128,4096]{1,0:T(8,128)(2,1)S(1)}, u32[]{:S(2)}, u32[]{:S(2)}) collective-permute-start(bf16[128,4096]{1,0:T(8,128)(2,1)S(1)} %add_convert_fusion.near_ref), channel_id=1, source_target_pairs={{0,2},{2,0},{1,3},{3,1},{4,6},{6,4},{5,7},{7,5},{8,10},{10,8},{9,1... | collective-permute-start | bytes 3145736 | tf_op jit(solution)/shard_map/ppermute | solution.py:57
  98.3 4.4 %collective-permute-start.12 = (bf16[272,512]{1,0:T(8,128)(2,1)S(1)}, bf16[272,512]{1,0:T(8,128)(2,1)S(1)}, u32[]{:S(2)}, u32[]{:S(2)}) collective-permute-start(bf16[272,512]{1,0:T(8,128)(2,1)S(1)} %collective-permute-done.6.refs_2_), channel_id=1, source_target_pairs={{4,8},{12,16},{20,24},{28,32},{36,40},{44,48},{52,56},{60,64},{68,... | collective-permute-start | bytes 835592 | tf_op jit(solution)/shard_map/ppermute | solution.py:67
  102.7 2.4 %convolution_convert_fusion = bf16[256,4096]{1,0:T(8,128)(2,1)S(1)} fusion(bf16[256,1024]{1,0:T(8,128)(2,1)S(1)} %get-tuple-element.69, bf16[1024,4096]{1,0:T(8,128)(2,1)S(1)} %bitcast.42), kind=kOutput, calls=%fused_computation | convolution fusion | flops 2148532224 | bytes 11010048 | tf_op jit(solution)/shard_map/dot_general | solution.py:45
  105.8 5.0 %collective-permute-done.12.refs_2_ = bf16[272,512]{1,0:T(8,128)(2,1)S(1)} collective-permute-done((bf16[272,512]{1,0:T(8,128)(2,1)S(1)}, bf16[272,512]{1,0:T(8,128)(2,1)S(1)}, u32[]{:S(2)}, u32[]{:S(2)}) %collective-permute-start.12) | collective-permute-done | bytes 278560 | tf_op jit(solution)/shard_map/ppermute | solution.py:67
  110.8 16.7 %collective-permute-done.10.far_ref = bf16[128,4096]{1,0:T(8,128)(2,1)S(1)} collective-permute-done((bf16[128,4096]{1,0:T(8,128)(2,1)S(1)}, bf16[128,4096]{1,0:T(8,128)(2,1)S(1)}, u32[]{:S(2)}, u32[]{:S(2)}) %collective-permute-start.10) | collective-permute-done | bytes 1048608 | tf_op jit(solution)/shard_map/ppermute | solution.py:57
  127.5 1.5 shard_map.151.own_ref
  129.0 1.1 slice.16
  130.1 1.2 collective-permute-start.14
  131.3 4.1 %collective-permute-done.14 = bf16[128,4096]{1,0:T(8,128)(2,1)} collective-permute-done((bf16[128,4096]{1,0:T(8,128)(2,1)}, bf16[128,4096]{1,0:T(8,128)(2,1)}, u32[]{:S(2)}, u32[]{:S(2)}) %collective-permute-start.14) | collective-permute-done | bytes 1048608 | tf_op jit(solution)/shard_map/ppermute | solution.py:53
  135.4 2.2 %copy-done.3 = bf16[512,4096]{1,0:T(8,128)(2,1)S(1)} copy-done((bf16[512,4096]{1,0:T(8,128)(2,1)S(1)}, bf16[512,4096]{1,0:T(8,128)(2,1)}, u32[]{:S(2)}) %copy-start.3) | copy-done | bytes 4194328
  137.6 0.9 copy-done.14
  138.5 1.5 shard_map.152
  140.0 5.2 %collective-permute-start.17 = (bf16[272,512]{1,0:T(8,128)(2,1)S(1)}, bf16[272,512]{1,0:T(8,128)(2,1)S(1)}, u32[]{:S(2)}, u32[]{:S(2)}) collective-permute-start(bf16[272,512]{1,0:T(8,128)(2,1)S(1)} %get-tuple-element.82.do_pack.refs_1_), channel_id=1, source_target_pairs={{4,8},{12,16},{20,24},{28,32},{36,40},{44,48},{52,56},{60,64},{68,... | collective-permute-start | bytes 835592 | tf_op jit(solution)/shard_map/ppermute | solution.py:67
  145.4 1.5 convert_add_fusion
  147.0 2.7 %collective-permute-start.15 = (bf16[64,4096]{1,0:T(8,128)(2,1)S(1)}, bf16[64,4096]{1,0:T(8,128)(2,1)S(1)}, u32[]{:S(2)}, u32[]{:S(2)}) collective-permute-start(bf16[64,4096]{1,0:T(8,128)(2,1)S(1)} %select_convert_fusion), channel_id=1, source_target_pairs={{0,2},{2,0},{1,3},{3,1},{4,6},{6,4},{5,7},{7,5},{8,10},{10,8},{9,1... | collective-permute-start | bytes 1572872 | tf_op jit(solution)/shard_map/ppermute | solution.py:57
  150.2 1.1 dynamic-slice_convert_fusion
  151.3 1.7 collective-permute-done.17.refs_5_
  153.1 4.8 %collective-permute-start.19 = (bf16[272,512]{1,0:T(8,128)(2,1)S(1)}, bf16[272,512]{1,0:T(8,128)(2,1)S(1)}, u32[]{:S(2)}, u32[]{:S(2)}) collective-permute-start(bf16[272,512]{1,0:T(8,128)(2,1)S(1)} %collective-permute-done.16.refs_3_), channel_id=1, source_target_pairs={{4,8},{12,16},{20,24},{28,32},{36,40},{44,48},{52,56},{60,64},{68,... | collective-permute-start | bytes 835592 | tf_op jit(solution)/shard_map/ppermute | solution.py:67
  158.0 2.7 %shard_map.154 = (f32[256,512]{1,0:T(8,128)S(1)}, f32[256,512]{1,0:T(8,128)S(1)}) custom-call(bf16[272,512]{1,0:T(8,128)(2,1)S(1)} %get-tuple-element.58.q_pack.refs_0_, bf16[272,512]{1,0:T(8,128)(2,1)S(1)} %get-tuple-element.82.do_pack.refs_1_, bf16[272,512]{1,0:T(8,128)(2,1)S(1)} %copy-done.18, bf16[272,512]{1,0:T(8,128)(2,1)S(1)} %collective-permute-done.16.refs_3_, ...), custom_call_target="tpu_custom_call" | custom-call | flops 1024 | bytes 1024 | tf_op jit(solution)/shard_map/pallas_call | solution.py:424
  160.7 5.6 %shard_map.153 = f32[256,512]{1,0:T(8,128)} custom-call(s32[3]{0:T(128)S(1)} %pad_add_fusion.place, bf16[272,512]{1,0:T(8,128)(2,1)S(1)} %get-tuple-element.58.q_pack.refs_0_, bf16[272,512]{1,0:T(8,128)(2,1)S(1)} %get-tuple-element.82.do_pack.refs_1_, f32[256,128]{1,0:T(8,128)S(1)} %copy-done.26, f32[256,128]{1,0:T(8,128)S(1)} %get-tuple-element.84.delta_ref, ...), custom_call_target="tpu_custom_call" | custom-call | flops 1024 | bytes 1024 | tf_op jit(solution)/shard_map/pallas_call | solution.py:417
  166.3 6.7 %collective-permute-done.15 = bf16[64,4096]{1,0:T(8,128)(2,1)S(1)} collective-permute-done((bf16[64,4096]{1,0:T(8,128)(2,1)S(1)}, bf16[64,4096]{1,0:T(8,128)(2,1)S(1)}, u32[]{:S(2)}, u32[]{:S(2)}) %collective-permute-start.15) | collective-permute-done | bytes 524320 | tf_op jit(solution)/shard_map/ppermute | solution.py:57
  173.0 1.2 add_add_fusion
  174.2 2.8 %shard_map.155 = (f32[256,512]{1,0:T(8,128)}, f32[256,512]{1,0:T(8,128)}) custom-call(bf16[272,512]{1,0:T(8,128)(2,1)S(1)} %copy-done.20, bf16[272,512]{1,0:T(8,128)(2,1)S(1)} %collective-permute-done.18.refs_1_, bf16[272,512]{1,0:T(8,128)(2,1)S(1)} %copy-done.22, bf16[272,512]{1,0:T(8,128)(2,1)S(1)} %collective-permute-done.19.refs_3_, ...), custom_call_target="tpu_custom_call" | custom-call | flops 1024 | bytes 1024 | tf_op jit(solution)/shard_map/pallas_call | solution.py:424
  (95 shorter events, 4.4 us)
Async XLA Ops:
  0.6 19.0 %copy-start = (bf16[256,4096]{1,0:T(8,128)(2,1)S(1)}, bf16[256,4096]{1,0:T(8,128)(2,1)}, u32[]{:S(2)}) copy-start(bf16[256,4096]{1,0:T(8,128)(2,1)} %param.14) | copy-start | bytes 6291460
  1.9 18.3 %collective-permute-start.1 = (bf16[2,256,512]{2,1,0:T(8,128)(2,1)S(1)}, bf16[2,256,512]{2,1,0:T(8,128)(2,1)S(1)}, u32[]{:S(2)}, u32[]{:S(2)}) collective-permute-start(bf16[2,256,512]{2,1,0:T(8,128)(2,1)S(1)} %pad_maximum_fusion.1), channel_id=1, source_target_pairs={{4,8},{12,16},{20,24},{28,32},{36,40},{44,48},{52,56},{60,64},{68,... | collective-permute-start | bytes 1572872 | tf_op jit(solution)/shard_map/ppermute | solution.py:67
  8.5 12.7 %collective-permute-start = (bf16[2,256,512]{2,1,0:T(8,128)(2,1)S(1)}, bf16[2,256,512]{2,1,0:T(8,128)(2,1)}, u32[]{:S(2)}, u32[]{:S(2)}) collective-permute-start(bf16[2,256,512]{2,1,0:T(8,128)(2,1)S(1)} %pad_maximum_fusion.1), channel_id=1, source_target_pairs={{0,4},{8,12},{16,20},{24,28},{32,36},{40,44},{48,52},{56,60},{64,6... | collective-permute-start | bytes 1572872 | tf_op jit(solution)/shard_map/ppermute | solution.py:67
  21.2 16.7 %collective-permute-start.3 = (bf16[2,256,512]{2,1,0:T(8,128)(2,1)}, bf16[2,256,512]{2,1,0:T(8,128)(2,1)S(1)}, u32[]{:S(2)}, u32[]{:S(2)}) collective-permute-start(bf16[2,256,512]{2,1,0:T(8,128)(2,1)} %collective-permute-done.kv_a), channel_id=1, source_target_pairs={{4,8},{12,16},{20,24},{28,32},{36,40},{44,48},{52,56},{60,64},{68,... | collective-permute-start | bytes 1572872 | tf_op jit(solution)/shard_map/ppermute | solution.py:67
  26.2 11.7 %collective-permute-start.2 = (bf16[2,256,512]{2,1,0:T(8,128)(2,1)S(1)}, bf16[2,256,512]{2,1,0:T(8,128)(2,1)S(1)}, u32[]{:S(2)}, u32[]{:S(2)}) collective-permute-start(bf16[2,256,512]{2,1,0:T(8,128)(2,1)S(1)} %collective-permute-done.1.kv_b), channel_id=1, source_target_pairs={{0,4},{8,12},{16,20},{24,28},{32,36},{40,44},{48,52},{56,60},{64,6... | collective-permute-start | bytes 1572872 | tf_op jit(solution)/shard_map/ppermute | solution.py:67
  26.5 11.4 %copy-start.5 = (bf16[256,512]{1,0:T(8,128)(2,1)S(1)}, bf16[256,512]{1,0:T(8,128)(2,1)}, u32[]{:S(2)}) copy-start(bf16[256,512]{1,0:T(8,128)(2,1)} %refs_4_.1) | copy-start | bytes 786436
  26.5 11.4 %copy-start.6 = (bf16[256,512]{1,0:T(8,128)(2,1)S(1)}, bf16[256,512]{1,0:T(8,128)(2,1)}, u32[]{:S(2)}) copy-start(bf16[256,512]{1,0:T(8,128)(2,1)} %refs_5_.1) | copy-start | bytes 786436
  26.5 11.4 %copy-start.23 = (bf16[256,512]{1,0:T(8,128)(2,1)S(1)}, bf16[256,512]{1,0:T(8,128)(2,1)}, u32[]{:S(2)}) copy-start(bf16[256,512]{1,0:T(8,128)(2,1)} %q_ref.1) | copy-start | bytes 786436
  26.5 15.4 %copy-start.2 = (bf16[512,4096]{1,0:T(8,128)(2,1)S(1)}, bf16[512,4096]{1,0:T(8,128)(2,1)}, u32[]{:S(2)}) copy-start(bf16[512,4096]{1,0:T(8,128)(2,1)} %weight_ref.3) | copy-start | bytes 12582916
  27.6 57.7 %slice-start = ((s8[8388608]{0:T(1024)(128)(4,1)}), s8[4194304]{0:T(1024)(128)(4,1)S(1)}, s32[]{:S(2)}) async-start(s8[8388608]{0:T(1024)(128)(4,1)} %bitcast.25), calls=%async_computation | async-start | bytes 8388608
  37.8 5.3 %copy-start.9 = (bf16[2,256,512]{2,1,0:T(8,128)(2,1)}, bf16[2,256,512]{2,1,0:T(8,128)(2,1)S(1)}, u32[]{:S(2)}) copy-start(bf16[2,256,512]{2,1,0:T(8,128)(2,1)S(1)} %collective-permute-done.3.kv_d) | copy-start | bytes 1572868
  37.9 5.3 %copy-start.11 = (bf16[2,256,512]{2,1,0:T(8,128)(2,1)}, bf16[2,256,512]{2,1,0:T(8,128)(2,1)S(1)}, u32[]{:S(2)}) copy-start(bf16[2,256,512]{2,1,0:T(8,128)(2,1)S(1)} %collective-permute-done.2.kv_c) | copy-start | bytes 1572868
  41.9 43.5 %slice-start.1 = ((s8[8388608]{0:T(1024)(128)(4,1)}), s8[4194304]{0:T(1024)(128)(4,1)S(1)}, s32[]{:S(2)}) async-start(s8[8388608]{0:T(1024)(128)(4,1)} %bitcast.25), calls=%async_computation.1 | async-start | bytes 8388608
  43.2 37.4 %copy-start.24 = (f32[4096]{0:T(1024)S(1)}, f32[4096]{0:T(1024)}, u32[]{:S(2)}) copy-start(f32[4096]{0:T(1024)} %param.16) | copy-start | bytes 49156
  43.2 5.2 %collective-permute-start.4 = (bf16[128,4096]{1,0:T(8,128)(2,1)S(1)}, bf16[128,4096]{1,0:T(8,128)(2,1)S(1)}, u32[]{:S(2)}, u32[]{:S(2)}) collective-permute-start(bf16[128,4096]{1,0:T(8,128)(2,1)S(1)} %get-tuple-element.56), channel_id=1, source_target_pairs={{0,1},{1,0},{2,3},{3,2},{4,5},{5,4},{6,7},{7,6},{8,9},{9,8},{10,11... | collective-permute-start | bytes 3145736 | tf_op jit(solution)/shard_map/ppermute | solution.py:53
  48.7 36.7 %copy-start.4 = (bf16[1024,1024]{1,0:T(8,128)(2,1)S(1)}, bf16[1024,1024]{1,0:T(8,128)(2,1)}, u32[]{:S(2)}) copy-start(bf16[1024,1024]{1,0:T(8,128)(2,1)} %fusion.2.pick_ref) | copy-start | bytes 6291460
  48.7 31.9 %collective-permute-start.5 = (bf16[128,4096]{1,0:T(8,128)(2,1)S(1)}, bf16[128,4096]{1,0:T(8,128)(2,1)S(1)}, u32[]{:S(2)}, u32[]{:S(2)}) collective-permute-start(bf16[128,4096]{1,0:T(8,128)(2,1)S(1)} %add_convert_fusion.1.near_ref), channel_id=1, source_target_pairs={{0,2},{2,0},{1,3},{3,1},{4,6},{6,4},{5,7},{7,5},{8,10},{10,8},{9,1... | collective-permute-start | bytes 3145736 | tf_op jit(solution)/shard_map/ppermute | solution.py:57
  51.4 12.5 %collective-permute-start.7 = (bf16[272,512]{1,0:T(8,128)(2,1)S(1)}, bf16[272,512]{1,0:T(8,128)(2,1)S(1)}, u32[]{:S(2)}, u32[]{:S(2)}) collective-permute-start(bf16[272,512]{1,0:T(8,128)(2,1)S(1)} %get-tuple-element.58.q_pack.refs_0_), channel_id=1, source_target_pairs={{4,8},{12,16},{20,24},{28,32},{36,40},{44,48},{52,56},{60,64},{68,... | collective-permute-start | bytes 835592 | tf_op jit(solution)/shard_map/ppermute | solution.py:67
  55.8 8.1 %collective-permute-start.6 = (bf16[272,512]{1,0:T(8,128)(2,1)S(1)}, bf16[272,512]{1,0:T(8,128)(2,1)S(1)}, u32[]{:S(2)}, u32[]{:S(2)}) collective-permute-start(bf16[272,512]{1,0:T(8,128)(2,1)S(1)} %get-tuple-element.58.q_pack.refs_0_), channel_id=1, source_target_pairs={{0,4},{8,12},{16,20},{24,28},{32,36},{40,44},{48,52},{56,60},{64,6... | collective-permute-start | bytes 835592 | tf_op jit(solution)/shard_map/ppermute | solution.py:67
  63.9 34.4 %copy-start.15 = (bf16[272,512]{1,0:T(8,128)(2,1)}, bf16[272,512]{1,0:T(8,128)(2,1)S(1)}, u32[]{:S(2)}) copy-start(bf16[272,512]{1,0:T(8,128)(2,1)S(1)} %collective-permute-done.7.refs_4_) | copy-start | bytes 835588
  63.9 34.4 %copy-start.17 = (bf16[272,512]{1,0:T(8,128)(2,1)}, bf16[272,512]{1,0:T(8,128)(2,1)S(1)}, u32[]{:S(2)}) copy-start(bf16[272,512]{1,0:T(8,128)(2,1)S(1)} %collective-permute-done.6.refs_2_) | copy-start | bytes 835588
  81.8 45.7 %copy-start.7 = (f32[128,4096]{1,0:T(8,128)}, f32[128,4096]{1,0:T(8,128)S(1)}, u32[]{:S(2)}) copy-start(f32[128,4096]{1,0:T(8,128)S(1)} %get-tuple-element.61.unit_ref) | copy-start | bytes 6291460
  81.8 3.6 %collective-permute-start.8 = (bf16[128,4096]{1,0:T(8,128)(2,1)S(1)}, bf16[128,4096]{1,0:T(8,128)(2,1)S(1)}, u32[]{:S(2)}, u32[]{:S(2)}) collective-permute-start(bf16[128,4096]{1,0:T(8,128)(2,1)S(1)} %get-tuple-element.62.own_ref), channel_id=1, source_target_pairs={{0,1},{1,0},{2,3},{3,2},{4,5},{5,4},{6,7},{7,6},{8,9},{9,8},{10,11... | collective-permute-start | bytes 3145736 | tf_op jit(solution)/shard_map/ppermute | solution.py:53
  85.4 17.4 %slice-start.2 = ((s8[8388608]{0:T(1024)(128)(4,1)}), s8[4194304]{0:T(1024)(128)(4,1)S(1)}, s32[]{:S(2)}) async-start(s8[8388608]{0:T(1024)(128)(4,1)} %bitcast.41), calls=%async_computation.2 | async-start | bytes 8388608
  85.4 17.3 %slice-start.3 = ((s8[8388608]{0:T(1024)(128)(4,1)}), s8[4194304]{0:T(1024)(128)(4,1)S(1)}, s32[]{:S(2)}) async-start(s8[8388608]{0:T(1024)(128)(4,1)} %bitcast.41), calls=%async_computation.3 | async-start | bytes 8388608
  92.6 2.7 %collective-permute-start.9 = (bf16[128,4096]{1,0:T(8,128)(2,1)S(1)}, bf16[128,4096]{1,0:T(8,128)(2,1)S(1)}, u32[]{:S(2)}, u32[]{:S(2)}) collective-permute-start(bf16[128,4096]{1,0:T(8,128)(2,1)S(1)} %get-tuple-element.68), channel_id=1, source_target_pairs={{0,1},{1,0},{2,3},{3,2},{4,5},{5,4},{6,7},{7,6},{8,9},{9,8},{10,11... | collective-permute-start | bytes 3145736 | tf_op jit(solution)/shard_map/ppermute | solution.py:53
  95.6 31.9 %collective-permute-start.10 = (bf16[128,4096]{1,0:T(8,128)(2,1)S(1)}, bf16[128,4096]{1,0:T(8,128)(2,1)S(1)}, u32[]{:S(2)}, u32[]{:S(2)}) collective-permute-start(bf16[128,4096]{1,0:T(8,128)(2,1)S(1)} %add_convert_fusion.near_ref), channel_id=1, source_target_pairs={{0,2},{2,0},{1,3},{3,1},{4,6},{6,4},{5,7},{7,5},{8,10},{10,8},{9,1... | collective-permute-start | bytes 3145736 | tf_op jit(solution)/shard_map/ppermute | solution.py:57
  98.3 7.5 %collective-permute-start.11 = (bf16[272,512]{1,0:T(8,128)(2,1)S(1)}, bf16[272,512]{1,0:T(8,128)(2,1)S(1)}, u32[]{:S(2)}, u32[]{:S(2)}) collective-permute-start(bf16[272,512]{1,0:T(8,128)(2,1)S(1)} %collective-permute-done.7.refs_4_), channel_id=1, source_target_pairs={{0,4},{8,12},{16,20},{24,28},{32,36},{40,44},{48,52},{56,60},{64,6... | collective-permute-start | bytes 835592 | tf_op jit(solution)/shard_map/ppermute | solution.py:67
  98.3 12.5 %collective-permute-start.12 = (bf16[272,512]{1,0:T(8,128)(2,1)S(1)}, bf16[272,512]{1,0:T(8,128)(2,1)S(1)}, u32[]{:S(2)}, u32[]{:S(2)}) collective-permute-start(bf16[272,512]{1,0:T(8,128)(2,1)S(1)} %collective-permute-done.6.refs_2_), channel_id=1, source_target_pairs={{4,8},{12,16},{20,24},{28,32},{36,40},{44,48},{52,56},{60,64},{68,... | collective-permute-start | bytes 835592 | tf_op jit(solution)/shard_map/ppermute | solution.py:67
  105.2 23.8 %copy-start.28 = (bf16[256,4096]{1,0:T(8,128)(2,1)}, bf16[256,4096]{1,0:T(8,128)(2,1)S(1)}, u32[]{:S(2)}) copy-start(bf16[256,4096]{1,0:T(8,128)(2,1)S(1)} %convolution_convert_fusion) | copy-start | bytes 6291460
  105.8 23.2 %copy-start.19 = (bf16[272,512]{1,0:T(8,128)(2,1)}, bf16[272,512]{1,0:T(8,128)(2,1)S(1)}, u32[]{:S(2)}) copy-start(bf16[272,512]{1,0:T(8,128)(2,1)S(1)} %collective-permute-done.11.refs_0_) | copy-start | bytes 835588
  110.8 18.2 %copy-start.21 = (bf16[272,512]{1,0:T(8,128)(2,1)}, bf16[272,512]{1,0:T(8,128)(2,1)S(1)}, u32[]{:S(2)}) copy-start(bf16[272,512]{1,0:T(8,128)(2,1)S(1)} %collective-permute-done.12.refs_2_) | copy-start | bytes 835588
  130.1 5.3 %collective-permute-start.14 = (bf16[128,4096]{1,0:T(8,128)(2,1)}, bf16[128,4096]{1,0:T(8,128)(2,1)}, u32[]{:S(2)}, u32[]{:S(2)}) collective-permute-start(bf16[128,4096]{1,0:T(8,128)(2,1)} %slice.16), channel_id=1, source_target_pairs={{0,1},{1,0},{2,3},{3,2},{4,5},{5,4},{6,7},{7,6},{8,9},{9,8},{10,11... | collective-permute-start | bytes 3145736 | tf_op jit(solution)/shard_map/ppermute | solution.py:53
  131.3 4.1 %collective-permute-start.13 = (bf16[128,4096]{1,0:T(8,128)(2,1)S(1)}, bf16[128,4096]{1,0:T(8,128)(2,1)S(1)}, u32[]{:S(2)}, u32[]{:S(2)}) collective-permute-start(bf16[128,4096]{1,0:T(8,128)(2,1)S(1)} %shard_map.151.own_ref), channel_id=1, source_target_pairs={{0,1},{1,0},{2,3},{3,2},{4,5},{5,4},{6,7},{7,6},{8,9},{9,8},{10,11... | collective-permute-start | bytes 3145736 | tf_op jit(solution)/shard_map/ppermute | solution.py:53
  140.0 5.4 %copy-start.29 = (bf16[256,4096]{1,0:T(8,128)(2,1)S(1)}, bf16[256,4096]{1,0:T(8,128)(2,1)}, u32[]{:S(2)}) copy-start(bf16[256,4096]{1,0:T(8,128)(2,1)} %copy-done.28) | copy-start | bytes 6291460
  140.0 12.9 %collective-permute-start.17 = (bf16[272,512]{1,0:T(8,128)(2,1)S(1)}, bf16[272,512]{1,0:T(8,128)(2,1)S(1)}, u32[]{:S(2)}, u32[]{:S(2)}) collective-permute-start(bf16[272,512]{1,0:T(8,128)(2,1)S(1)} %get-tuple-element.82.do_pack.refs_1_), channel_id=1, source_target_pairs={{4,8},{12,16},{20,24},{28,32},{36,40},{44,48},{52,56},{60,64},{68,... | collective-permute-start | bytes 835592 | tf_op jit(solution)/shard_map/ppermute | solution.py:67
  145.2 7.8 %collective-permute-start.16 = (bf16[272,512]{1,0:T(8,128)(2,1)S(1)}, bf16[272,512]{1,0:T(8,128)(2,1)S(1)}, u32[]{:S(2)}, u32[]{:S(2)}) collective-permute-start(bf16[272,512]{1,0:T(8,128)(2,1)S(1)} %get-tuple-element.82.do_pack.refs_1_), channel_id=1, source_target_pairs={{0,4},{8,12},{16,20},{24,28},{32,36},{40,44},{48,52},{56,60},{64,6... | collective-permute-start | bytes 835592 | tf_op jit(solution)/shard_map/ppermute | solution.py:67
  147.0 26.0 %collective-permute-start.15 = (bf16[64,4096]{1,0:T(8,128)(2,1)S(1)}, bf16[64,4096]{1,0:T(8,128)(2,1)S(1)}, u32[]{:S(2)}, u32[]{:S(2)}) collective-permute-start(bf16[64,4096]{1,0:T(8,128)(2,1)S(1)} %select_convert_fusion), channel_id=1, source_target_pairs={{0,2},{2,0},{1,3},{3,1},{4,6},{6,4},{5,7},{7,5},{8,10},{10,8},{9,1... | collective-permute-start | bytes 1572872 | tf_op jit(solution)/shard_map/ppermute | solution.py:57
  149.9 8.1 %copy-start.16 = (bf16[272,512]{1,0:T(8,128)(2,1)S(1)}, bf16[272,512]{1,0:T(8,128)(2,1)}, u32[]{:S(2)}) copy-start(bf16[272,512]{1,0:T(8,128)(2,1)} %copy-done.15) | copy-start | bytes 835588
  149.9 8.1 %copy-start.18 = (bf16[272,512]{1,0:T(8,128)(2,1)S(1)}, bf16[272,512]{1,0:T(8,128)(2,1)}, u32[]{:S(2)}) copy-start(bf16[272,512]{1,0:T(8,128)(2,1)} %copy-done.17) | copy-start | bytes 835588
  150.1 10.5 %copy-start.10 = (bf16[2,256,512]{2,1,0:T(8,128)(2,1)S(1)}, bf16[2,256,512]{2,1,0:T(8,128)(2,1)}, u32[]{:S(2)}) copy-start(bf16[2,256,512]{2,1,0:T(8,128)(2,1)} %copy-done.9) | copy-start | bytes 1572868
  150.2 10.5 %copy-start.12 = (bf16[2,256,512]{2,1,0:T(8,128)(2,1)S(1)}, bf16[2,256,512]{2,1,0:T(8,128)(2,1)}, u32[]{:S(2)}) copy-start(bf16[2,256,512]{2,1,0:T(8,128)(2,1)} %copy-done.11) | copy-start | bytes 1572868
  150.2 10.5 %copy-start.26 = (f32[256,128]{1,0:T(8,128)S(1)}, f32[256,128]{1,0:T(8,128)}, u32[]{:S(2)}) copy-start(f32[256,128]{1,0:T(8,128)} %copy-done.25) | copy-start | bytes 393220
  152.9 21.3 %collective-permute-start.18 = (bf16[272,512]{1,0:T(8,128)(2,1)S(1)}, bf16[272,512]{1,0:T(8,128)(2,1)S(1)}, u32[]{:S(2)}, u32[]{:S(2)}) collective-permute-start(bf16[272,512]{1,0:T(8,128)(2,1)S(1)} %collective-permute-done.17.refs_5_), channel_id=1, source_target_pairs={{0,4},{8,12},{16,20},{24,28},{32,36},{40,44},{48,52},{56,60},{64,6... | collective-permute-start | bytes 835592 | tf_op jit(solution)/shard_map/ppermute | solution.py:67
  153.1 21.1 %collective-permute-start.19 = (bf16[272,512]{1,0:T(8,128)(2,1)S(1)}, bf16[272,512]{1,0:T(8,128)(2,1)S(1)}, u32[]{:S(2)}, u32[]{:S(2)}) collective-permute-start(bf16[272,512]{1,0:T(8,128)(2,1)S(1)} %collective-permute-done.16.refs_3_), channel_id=1, source_target_pairs={{4,8},{12,16},{20,24},{28,32},{36,40},{44,48},{52,56},{60,64},{68,... | collective-permute-start | bytes 835592 | tf_op jit(solution)/shard_map/ppermute | solution.py:67
  160.7 12.4 %copy-start.8 = (f32[128,4096]{1,0:T(8,128)S(1)}, f32[128,4096]{1,0:T(8,128)}, u32[]{:S(2)}) copy-start(f32[128,4096]{1,0:T(8,128)} %copy-done.7) | copy-start | bytes 6291460
  166.3 7.9 %copy-start.20 = (bf16[272,512]{1,0:T(8,128)(2,1)S(1)}, bf16[272,512]{1,0:T(8,128)(2,1)}, u32[]{:S(2)}) copy-start(bf16[272,512]{1,0:T(8,128)(2,1)} %copy-done.19) | copy-start | bytes 835588
  166.3 7.9 %copy-start.22 = (bf16[272,512]{1,0:T(8,128)(2,1)S(1)}, bf16[272,512]{1,0:T(8,128)(2,1)}, u32[]{:S(2)}) copy-start(bf16[272,512]{1,0:T(8,128)(2,1)} %copy-done.21) | copy-start | bytes 835588
  (6 other events, 11.1 us)

commit v2 on v1

--- a/solution.py
+++ b/solution.py
@@ -22,7 +22,6 @@
 
 VMEM = pl.BlockSpec(memory_space=pltpu.VMEM)
 SMEM = pl.BlockSpec(memory_space=pltpu.SMEM)
-ANY = pl.BlockSpec(memory_space=pl.ANY)
 
 
 def call(kernel, out_shape, in_specs, scratch=()):
@@ -228,11 +227,15 @@
         other_ref[:, start : start + OUT_STEP] = product[rows:]
 
 
+def grad_attended_own_kernel(low_ref, weight_ref, grad_ref):
+    grad_ref[...] = dot_nt(low_ref[...], weight_ref[...]).astype(BF16)
+
+
 def grad_attended_kernel(own_ref, near_ref, weight_ref, att_ref, pack_ref, delta_ref):
     rows, width = att_ref.shape
     heads = width // HEAD_DIM
-    low = jnp.concatenate([own_ref[...], near_ref[...]], axis=0)
-    pack_ref[:rows] = dot_nt(low, weight_ref[...]).astype(BF16)
+    pack_ref[: rows // 2] = own_ref[...]
+    pack_ref[rows // 2 : rows] = dot_nt(near_ref[...], weight_ref[...]).astype(BF16)
     product = pack_ref[:rows].astype(F32) * att_ref[...].astype(F32)
     lane = lax.broadcasted_iota(jnp.int32, (rows, HEAD_DIM), 1)
     delta = jnp.zeros((rows, HEAD_DIM), F32)
@@ -362,15 +365,16 @@
         [SMEM] + [VMEM] * 7,
     )(place, query_heads, *window)
 
-    def chip_sum(kernel, operands):
-        own, other = call(kernel, (shape((half, model_width), BF16),) * 2, [VMEM, VMEM])(*operands)
-        near = (own.astype(F32) + swap_core(other).astype(F32)).astype(BF16)
-        return near, swap_chip(near)
-
-    near, far = chip_sum(out_kernel, (attended, out_weight))
-
-    q_early = after(q_pack, near)
-    far, q_a, q_b = lax.optimization_barrier((far, swap_block(q_early, 0), swap_block(q_early, 1)))
+    def two_parts(kernel, operands):
+        return call(kernel, (shape((half, model_width), BF16),) * 2, [VMEM, VMEM])(*operands)
+
+    def chip_sum(own, other):
+        return own.astype(F32) + swap_core(other).astype(F32)
+
+    near = chip_sum(*two_parts(out_kernel, (attended, out_weight))).astype(BF16)
+    far = swap_chip(near)
+
+    far, q_a = lax.optimization_barrier((far, swap_block(after(q_pack, near), 0)))
 
     unit, sigma, normed = call(
         norm_kernel,
@@ -385,11 +389,17 @@
     merged, hidden_grad = call(ffn_kernel, (shape((rows, src_width), BF16),) * 2, [VMEM] * 8)(
         normed, near_normed, up_source, pick, grad_merged, grad_copy, inverse_row, copy_row
     )
-    near, far = chip_sum(back_kernel, (hidden_grad, up_source))
-    ffn_part = dot(merged, down_source).astype(BF16)
-    q_c, q_d = after((q_b, q_a), near)
-    q_c, q_d = swap_block(q_c, 0), swap_block(q_d, 1)
-    far, ffn_part, q_c, q_d = lax.optimization_barrier((far, ffn_part, q_c, q_d))
+    ffn_parts = two_parts(out_kernel, (merged, down_source))
+    hidden_grad, ffn_parts, q_b = lax.optimization_barrier(
+        (hidden_grad, ffn_parts, swap_block(after(q_pack, normed), 1))
+    )
+    near = chip_sum(*two_parts(back_kernel, (hidden_grad, up_source))).astype(BF16)
+    far = swap_chip(near)
+    ffn_chip = chip_sum(*ffn_parts).reshape(2, half // 2, model_width)
+    ffn_send = jnp.where(chip == 0, ffn_chip[1], ffn_chip[0]).astype(BF16)
+    ffn_mine = jnp.where(chip == 0, ffn_chip[0], ffn_chip[1])
+    q_c = swap_block(after(q_b, near), 0)
+    far, ffn_send, ffn_mine, q_c = lax.optimization_barrier((far, ffn_send, ffn_mine, q_c))
 
     low = call(
         norm_back_kernel,
@@ -397,21 +407,19 @@
         [VMEM] * 6,
         scratch=[pltpu.VMEM((half, model_width), F32)],
     )(near, far, cot_own, gain_row, unit, sigma)
-    ffn_part = after(ffn_part, low)
-    near_low, ffn_near = lax.optimization_barrier((swap_core(low), swap_core(ffn_part[half:])))
+    near_low = swap_core(low)
+    ffn_far = swap_chip(after(ffn_send, low))
+    grad_own = call(grad_attended_own_kernel, shape((half, head_width), BF16), [VMEM] * 2)(low, out_weight)
+    near_low, grad_own = lax.optimization_barrier((near_low, grad_own))
     do_pack, delta = call(
         grad_attended_kernel,
         (shape((rows + STAT_ROWS, head_width), BF16), shape((rows, HEAD_DIM), F32)),
         [VMEM] * 4,
-    )(low, near_low, out_weight, attended)
+    )(grad_own, near_low, out_weight, attended)
 
     do_a, do_b = swap_block(do_pack, 0), swap_block(do_pack, 1)
 
-    ffn_part = after(ffn_part, do_pack)
-    ffn_chip = (ffn_part[:half].astype(F32) + ffn_near.astype(F32)).reshape(2, half // 2, model_width)
-    ffn_far = swap_chip(jnp.where(chip == 0, ffn_chip[1], ffn_chip[0]).astype(BF16))
-    ffn_mine = jnp.where(chip == 0, ffn_chip[0], ffn_chip[1])
-
+    q_d = swap_block(after(q_a, do_pack), 1)
     do_a, do_b, do_own = lax.optimization_barrier((do_a, do_b, do_pack))
     do_c, do_d = swap_block(do_b, 0), swap_block(do_a, 1)
     grad_query = call(
@@ -429,7 +437,7 @@
 
     sums = grad_key_value([(q_pack, do_own), (q_a, do_a), (q_b, do_b)], ())
     own_unit = lax.dynamic_slice_in_dim(unit, chip * (half // 2), half // 2, 0)
-    encoded = own_unit * ln_gain + (ffn_mine + ffn_far.astype(F32))
+    encoded = own_unit * ln_gain + (ffn_mine + after(ffn_far, grad_query, *sums).astype(F32))
     grad_key, grad_value = grad_key_value([(q_c, do_c), (q_d, do_d)], sums)
 
     col_width = model_width // lax.axis_size("tp")

time: 178 us -> 169 us (0.949)
  waiting for transfers between devices: 76.9 us -> 62.9 us
  Pallas kernels: 27.5 us -> 33.4 us
  other arithmetic: 9.55 us -> 12.6 us
  matrix products: 10.3 us -> 8.25 us
    ppermute x5, waiting for transfers between devices: 11 us -> 4.92 us  [swap_core(): return lax.ppermute(array, 'tp', [(0, 1), (1, 0), (2, 3), (3, 2)])]
    ppermute x3, waiting for transfers between devices: 40.1 us -> 34 us  [swap_chip(): return lax.ppermute(array, 'tp', [(0, 2), (2, 0), (1, 3), (3, 1)])]
    pallas_call x2 -> x4, Pallas kernels: 3.64 us -> 9.44 us  [the longest x3 7.92 us: two_parts(): call(kernel, (shape((half, model_width), BF16),) * 2, [VMEM, VMEM])]
    dot_general x3 -> x2, matrix products: 4.53 us -> 2.13 us  [dot(): return jnp.dot(a, b, preferred_element_type=F32)]
    convert_element_type x3, other arithmetic: 0.59 us -> 2.6 us  [the longest x1 1.47 us: shards(): chip_sum(*two_parts(back_kernel, (hidden_grad, up_source))).astype(BF16)]
    ppermute x12, waiting for transfers between devices: 25.9 us -> 23.9 us  [swap_block(): return lax.ppermute(array, 'seq', ahead + [(j, i) for i, j in ahead])]
  transfers between devices with their start and end apart: 20 -> 20, of which waited for: 14 -> 11; matrix products, arithmetic and copies ran while one was open for 11% -> 13% of each run, Pallas kernels for 5% -> 12%
where the time goes in v2:
time: 169 us; the launch traced here: 168 us
  waiting for transfers between devices  62.9 us (37%)
  starting transfers between devices  44.4 us (26%)
  Pallas kernels  33.4 us (20%)
  other arithmetic  12.6 us (7%)
  matrix products  8.25 us (5%)
  local copies, waits for them, and re-layouts  5.04 us (3%)
    ppermute x3, waiting for transfers between devices, swap_chip(): return lax.ppermute(array, 'tp', [(0, 2), (2, 0), (1, 3), (3, 1)])  34 us
    ppermute x12, starting transfers between devices, swap_block(): return lax.ppermute(array, 'seq', ahead + [(j, i) for i, j in ahead])  30.1 us
    ppermute x12, waiting for transfers between devices, swap_block(): return lax.ppermute(array, 'seq', ahead + [(j, i) for i, j in ahead])  23.9 us
    ppermute x3, starting transfers between devices, swap_chip(): return lax.ppermute(array, 'tp', [(0, 2), (2, 0), (1, 3), (3, 1)])  8.1 us
    pallas_call x3, Pallas kernels, two_parts(): call(kernel, (shape((half, model_width), BF16),) * 2, [VMEM, VMEM])  7.92 us
    ppermute x5, starting transfers between devices, swap_core(): return lax.ppermute(array, 'tp', [(0, 1), (1, 0), (2, 3), (3, 2)])  6.13 us
    dot_general x1, matrix products, dot_nt(): return lax.dot_general(a, b, NT, preferred_element_type=F32)  6.12 us
    pallas_call x1, Pallas kernels, shards(): call(functools.partial(grad_query_kernel, scale), shape((rows, head_width...  5.58 us
  transfers between devices with their start and end apart: 20, of which 11 were waited for; matrix products, arithmetic and copies ran while one was open for 13% of the time, Pallas kernels for 12%

profile of v2, /device:TPU:5, one launch (start us, length us, event | category | flops | bytes accessed | tf_op | source)
XLA Modules:
  0.0 167.8 jit_solution(6105012267668043674)
XLA Ops:
  0.6 1.2 pad_maximum_fusion.1
  1.9 6.7 %collective-permute-start.1 = (bf16[2,256,512]{2,1,0:T(8,128)(2,1)S(1)}, bf16[2,256,512]{2,1,0:T(8,128)(2,1)S(1)}, u32[]{:S(2)}, u32[]{:S(2)}) collective-permute-start(bf16[2,256,512]{2,1,0:T(8,128)(2,1)S(1)} %pad_maximum_fusion.1), channel_id=1, source_target_pairs={{4,8},{12,16},{20,24},{28,32},{36,40},{44,48},{52,56},{60,64},{68,... | collective-permute-start | bytes 1572872 | tf_op jit(solution)/shard_map/ppermute | solution.py:66
  9.8 2.2 %fusion.2.pick_ref = bf16[1024,1024]{1,0:T(8,128)(2,1)} fusion(s32[1024]{0:T(1024)S(1)} %broadcast_subtract_fusion), kind=kLoop, calls=%fused_computation.4 | loop fusion | flops 2097152 | bytes 2101248 | tf_op jit(solution)/shard_map/convert_element_type | solution.py:344
  12.1 1.7 %constant_dynamic-slice_fusion.2 = (bf16[2,1,64,4096]{3,2,1,0:T(8,128)(2,1)S(1)}, bf16[2,1,64,4096]{3,2,1,0:T(8,128)(2,1)S(1)}) fusion(bf16[2,2,64,4096]{3,2,1,0:T(8,128)(2,1)} %bitcast.39, s32[]{:T(128)S(6)} %select_n.49, s32[]{:T(128)S(6)} %select_n.50), kind=kLoop, calls=%fused_computation.32 | loop fusion | bytes 4194312 | tf_op jit(solution)/shard_map/dynamic_slice | solution.py:332
  13.8 6.1 %fusion.3 = f32[256,1024]{1,0:T(8,128)S(1)} fusion(bf16[1024,4096]{1,0:T(8,128)(2,1)} %weight_ref.5, bf16[128,4096]{1,0:T(8,128)(2,1)S(1)} %bitcast.40, bf16[128,4096]{1,0:T(8,128)(2,1)S(1)} %bitcast.29), kind=kOutput, calls=%fused_computation.5 | convolution fusion | flops 2151677952 | bytes 11534336 | tf_op jit(solution)/shard_map/dot_general | solution.py:48
  20.2 1.0 collective-permute-done.kv_a
  21.2 5.0 %collective-permute-start.3 = (bf16[2,256,512]{2,1,0:T(8,128)(2,1)}, bf16[2,256,512]{2,1,0:T(8,128)(2,1)S(1)}, u32[]{:S(2)}, u32[]{:S(2)}) collective-permute-start(bf16[2,256,512]{2,1,0:T(8,128)(2,1)} %collective-permute-done.kv_a), channel_id=1, source_target_pairs={{4,8},{12,16},{20,24},{28,32},{36,40},{44,48},{52,56},{60,64},{68,... | collective-permute-start | bytes 1572872 | tf_op jit(solution)/shard_map/ppermute | solution.py:66
  26.5 1.1 fusion
  27.6 1.0 fusion.10.grad_copy_ref
  28.7 9.2 %collective-permute-done.3.kv_d = bf16[2,256,512]{2,1,0:T(8,128)(2,1)S(1)} collective-permute-done((bf16[2,256,512]{2,1,0:T(8,128)(2,1)}, bf16[2,256,512]{2,1,0:T(8,128)(2,1)S(1)}, u32[]{:S(2)}, u32[]{:S(2)}) %collective-permute-start.3) | collective-permute-done | bytes 524320 | tf_op jit(solution)/shard_map/ppermute | solution.py:66
  37.9 4.0 %shard_map.146 = (bf16[256,512]{1,0:T(8,128)(2,1)S(1)}, bf16[272,512]{1,0:T(8,128)(2,1)S(1)}, f32[256,128]{1,0:T(8,128)S(1)}) custom-call(s32[3]{0:T(128)S(1)} %pad_add_fusion.place, bf16[256,512]{1,0:T(8,128)(2,1)S(1)} %copy-done.26, bf16[256,512]{1,0:T(8,128)(2,1)S(1)} %copy-done.6, bf16[256,512]{1,0:T(8,128)(2,1)S(1)} %copy-done.7, ...), custom_call_target="tpu_custom_call" | custom-call | flops 1024 | bytes 1024 | tf_op jit(solution)/shard_map/pallas_call | solution.py:358
  41.9 1.3 shard_map.147
  43.3 2.9 %collective-permute-start.4 = (bf16[128,4096]{1,0:T(8,128)(2,1)S(1)}, bf16[128,4096]{1,0:T(8,128)(2,1)S(1)}, u32[]{:S(2)}, u32[]{:S(2)}) collective-permute-start(bf16[128,4096]{1,0:T(8,128)(2,1)S(1)} %get-tuple-element.62), channel_id=1, source_target_pairs={{0,1},{1,0},{2,3},{3,2},{4,5},{5,4},{6,7},{7,6},{8,9},{9,8},{10,11... | collective-permute-start | bytes 3145736 | tf_op jit(solution)/shard_map/ppermute | solution.py:52
  46.1 2.3 %collective-permute-done.4 = bf16[128,4096]{1,0:T(8,128)(2,1)S(1)} collective-permute-done((bf16[128,4096]{1,0:T(8,128)(2,1)S(1)}, bf16[128,4096]{1,0:T(8,128)(2,1)S(1)}, u32[]{:S(2)}, u32[]{:S(2)}) %collective-permute-start.4) | collective-permute-done | bytes 1048608 | tf_op jit(solution)/shard_map/ppermute | solution.py:52
  48.7 2.7 %collective-permute-start.5 = (bf16[128,4096]{1,0:T(8,128)(2,1)S(1)}, bf16[128,4096]{1,0:T(8,128)(2,1)S(1)}, u32[]{:S(2)}, u32[]{:S(2)}) collective-permute-start(bf16[128,4096]{1,0:T(8,128)(2,1)S(1)} %add_convert_fusion.1.near_ref), channel_id=1, source_target_pairs={{0,2},{2,0},{1,3},{3,1},{4,6},{6,4},{5,7},{7,5},{8,10},{10,8},{9,1... | collective-permute-start | bytes 3145736 | tf_op jit(solution)/shard_map/ppermute | solution.py:56
  51.4 7.5 %collective-permute-done.6.refs_2_ = bf16[272,512]{1,0:T(8,128)(2,1)S(1)} collective-permute-done((bf16[272,512]{1,0:T(8,128)(2,1)S(1)}, bf16[272,512]{1,0:T(8,128)(2,1)S(1)}, u32[]{:S(2)}, u32[]{:S(2)}) %collective-permute-start.6) | collective-permute-done | bytes 278560 | tf_op jit(solution)/shard_map/ppermute | solution.py:66
  59.0 15.7 %collective-permute-done.5.far_ref = bf16[128,4096]{1,0:T(8,128)(2,1)S(1)} collective-permute-done((bf16[128,4096]{1,0:T(8,128)(2,1)S(1)}, bf16[128,4096]{1,0:T(8,128)(2,1)S(1)}, u32[]{:S(2)}, u32[]{:S(2)}) %collective-permute-start.5) | collective-permute-done | bytes 1048608 | tf_op jit(solution)/shard_map/ppermute | solution.py:56
  74.7 1.2 shard_map.148
  75.8 1.3 collective-permute-start.7
  77.1 5.0 %collective-permute-start.8 = (bf16[272,512]{1,0:T(8,128)(2,1)S(1)}, bf16[272,512]{1,0:T(8,128)(2,1)S(1)}, u32[]{:S(2)}, u32[]{:S(2)}) collective-permute-start(bf16[272,512]{1,0:T(8,128)(2,1)S(1)} %get-tuple-element.76.q_pack.refs_0_), channel_id=1, source_target_pairs={{4,8},{12,16},{20,24},{28,32},{36,40},{44,48},{52,56},{60,64},{68,... | collective-permute-start | bytes 835592 | tf_op jit(solution)/shard_map/ppermute | solution.py:66
  82.2 4.8 %shard_map.149 = (bf16[256,1024]{1,0:T(8,128)(2,1)S(1)}, bf16[256,1024]{1,0:T(8,128)(2,1)S(1)}) custom-call(bf16[128,4096]{1,0:T(8,128)(2,1)S(1)} %get-tuple-element.68.own_ref, bf16[128,4096]{1,0:T(8,128)(2,1)S(1)} %collective-permute-done.7.near_ref, bf16[4096,1024]{1,0:T(8,128)(2,1)S(1)} %bitcast.24, bf16[1024,1024]{1,0:T(8,128)(2,1)S(1)} %copy-done.5, ...), custom_call_target="tpu_custom_call" | custom-call | flops 1024 | bytes 1024 | tf_op jit(solution)/shard_map/pallas_call | solution.py:389
  87.1 3.3 %shard_map.150 = (bf16[128,4096]{1,0:T(8,128)(2,1)S(1)}, bf16[128,4096]{1,0:T(8,128)(2,1)}) custom-call(bf16[256,1024]{1,0:T(8,128)(2,1)S(1)} %get-tuple-element.73.att_ref, bf16[1024,4096]{1,0:T(8,128)(2,1)S(1)} %bitcast.26), custom_call_target="tpu_custom_call" | custom-call | flops 1024 | bytes 1024 | tf_op jit(solution)/shard_map/pallas_call | solution.py:369
  90.4 3.3 %shard_map.151 = (bf16[128,4096]{1,0:T(8,128)(2,1)S(1)}, bf16[128,4096]{1,0:T(8,128)(2,1)}) custom-call(bf16[256,1024]{1,0:T(8,128)(2,1)S(1)} %get-tuple-element.77.hidden_grad_ref, bf16[4096,1024]{1,0:T(8,128)(2,1)S(1)} %bitcast.24), custom_call_target="tpu_custom_call" | custom-call | flops 1024 | bytes 1024 | tf_op jit(solution)/shard_map/pallas_call | solution.py:369
  94.4 2.6 %collective-permute-done.9 = bf16[128,4096]{1,0:T(8,128)(2,1)} collective-permute-done((bf16[128,4096]{1,0:T(8,128)(2,1)}, bf16[128,4096]{1,0:T(8,128)(2,1)}, u32[]{:S(2)}, u32[]{:S(2)}) %collective-permute-start.9) | collective-permute-done | bytes 1048608 | tf_op jit(solution)/shard_map/ppermute | solution.py:52
  97.1 1.5 add_convert_fusion.near_ref
  98.5 2.7 %collective-permute-start.10 = (bf16[128,4096]{1,0:T(8,128)(2,1)S(1)}, bf16[128,4096]{1,0:T(8,128)(2,1)S(1)}, u32[]{:S(2)}, u32[]{:S(2)}) collective-permute-start(bf16[128,4096]{1,0:T(8,128)(2,1)S(1)} %add_convert_fusion.near_ref), channel_id=1, source_target_pairs={{0,2},{2,0},{1,3},{3,1},{4,6},{6,4},{5,7},{7,5},{8,10},{10,8},{9,1... | collective-permute-start | bytes 3145736 | tf_op jit(solution)/shard_map/ppermute | solution.py:56
  101.2 1.5 convert_add_fusion
  102.7 1.1 slice_select_fusion
  103.8 0.9 select_convert_fusion
  104.7 4.1 %collective-permute-done.12.refs_0_ = bf16[272,512]{1,0:T(8,128)(2,1)S(1)} collective-permute-done((bf16[272,512]{1,0:T(8,128)(2,1)S(1)}, bf16[272,512]{1,0:T(8,128)(2,1)S(1)}, u32[]{:S(2)}, u32[]{:S(2)}) %collective-permute-start.12) | collective-permute-done | bytes 278560 | tf_op jit(solution)/shard_map/ppermute | solution.py:66
  108.8 15.7 %collective-permute-done.10.far_ref = bf16[128,4096]{1,0:T(8,128)(2,1)S(1)} collective-permute-done((bf16[128,4096]{1,0:T(8,128)(2,1)S(1)}, bf16[128,4096]{1,0:T(8,128)(2,1)S(1)}, u32[]{:S(2)}, u32[]{:S(2)}) %collective-permute-start.10) | collective-permute-done | bytes 1048608 | tf_op jit(solution)/shard_map/ppermute | solution.py:56
  124.5 1.3 shard_map.152.low_ref
  125.8 1.3 collective-permute-start.14
  127.1 2.2 %copy-done.3 = bf16[512,4096]{1,0:T(8,128)(2,1)S(1)} copy-done((bf16[512,4096]{1,0:T(8,128)(2,1)S(1)}, bf16[512,4096]{1,0:T(8,128)(2,1)}, u32[]{:S(2)}) %copy-start.3) | copy-done | bytes 4194328
  129.3 1.5 shard_map.153.own_ref
  130.8 2.7 %collective-permute-start.13 = (bf16[64,4096]{1,0:T(8,128)(2,1)S(1)}, bf16[64,4096]{1,0:T(8,128)(2,1)S(1)}, u32[]{:S(2)}, u32[]{:S(2)}) collective-permute-start(bf16[64,4096]{1,0:T(8,128)(2,1)S(1)} %copy-done.32), channel_id=1, source_target_pairs={{0,2},{2,0},{1,3},{3,1},{4,6},{6,4},{5,7},{7,5},{8,10},{10,8},{9,1... | collective-permute-start | bytes 1572872 | tf_op jit(solution)/shard_map/ppermute | solution.py:56
  133.5 1.7 %shard_map.154 = (bf16[272,512]{1,0:T(8,128)(2,1)S(1)}, f32[256,128]{1,0:T(8,128)S(1)}) custom-call(bf16[128,512]{1,0:T(8,128)(2,1)S(1)} %shard_map.153.own_ref, bf16[128,4096]{1,0:T(8,128)(2,1)S(1)} %collective-permute-done.14.near_ref, bf16[512,4096]{1,0:T(8,128)(2,1)S(1)} %copy-done.4, bf16[256,512]{1,0:T(8,128)(2,1)S(1)} %copy-done.18), custom_call_target="tpu_custom_call" | custom-call | flops 1024 | bytes 1024 | tf_op jit(solution)/shard_map/pallas_call | solution.py:414
  135.2 4.4 %collective-permute-start.16 = (bf16[272,512]{1,0:T(8,128)(2,1)S(1)}, bf16[272,512]{1,0:T(8,128)(2,1)S(1)}, u32[]{:S(2)}, u32[]{:S(2)}) collective-permute-start(bf16[272,512]{1,0:T(8,128)(2,1)S(1)} %get-tuple-element.92.do_pack.refs_1_), channel_id=1, source_target_pairs={{4,8},{12,16},{20,24},{28,32},{36,40},{44,48},{52,56},{60,64},{68,... | collective-permute-start | bytes 835592 | tf_op jit(solution)/shard_map/ppermute | solution.py:66
  140.3 0.8 copy-done.20
  141.1 4.0 %collective-permute-start.18 = (bf16[272,512]{1,0:T(8,128)(2,1)S(1)}, bf16[272,512]{1,0:T(8,128)(2,1)S(1)}, u32[]{:S(2)}, u32[]{:S(2)}) collective-permute-start(bf16[272,512]{1,0:T(8,128)(2,1)S(1)} %copy-done.20), channel_id=1, source_target_pairs={{4,8},{12,16},{20,24},{28,32},{36,40},{44,48},{52,56},{60,64},{68,... | collective-permute-start | bytes 835592 | tf_op jit(solution)/shard_map/ppermute | solution.py:66
  145.1 1.1 dynamic-slice_convert_fusion
  146.2 2.0 %collective-permute-done.16.refs_5_ = bf16[272,512]{1,0:T(8,128)(2,1)S(1)} collective-permute-done((bf16[272,512]{1,0:T(8,128)(2,1)S(1)}, bf16[272,512]{1,0:T(8,128)(2,1)S(1)}, u32[]{:S(2)}, u32[]{:S(2)}) %collective-permute-start.16) | collective-permute-done | bytes 278560 | tf_op jit(solution)/shard_map/ppermute | solution.py:66
  148.1 4.4 %collective-permute-start.19 = (bf16[272,512]{1,0:T(8,128)(2,1)S(1)}, bf16[272,512]{1,0:T(8,128)(2,1)S(1)}, u32[]{:S(2)}, u32[]{:S(2)}) collective-permute-start(bf16[272,512]{1,0:T(8,128)(2,1)S(1)} %collective-permute-done.15.refs_3_), channel_id=1, source_target_pairs={{4,8},{12,16},{20,24},{28,32},{36,40},{44,48},{52,56},{60,64},{68,... | collective-permute-start | bytes 835592 | tf_op jit(solution)/shard_map/ppermute | solution.py:66
  152.9 2.7 %shard_map.156 = (f32[256,512]{1,0:T(8,128)S(1)}, f32[256,512]{1,0:T(8,128)S(1)}) custom-call(bf16[272,512]{1,0:T(8,128)(2,1)S(1)} %get-tuple-element.76.q_pack.refs_0_, bf16[272,512]{1,0:T(8,128)(2,1)S(1)} %get-tuple-element.92.do_pack.refs_1_, bf16[272,512]{1,0:T(8,128)(2,1)S(1)} %copy-done.20, bf16[272,512]{1,0:T(8,128)(2,1)S(1)} %collective-permute-done.15.refs_3_, ...), custom_call_target="tpu_custom_call" | custom-call | flops 1024 | bytes 1024 | tf_op jit(solution)/shard_map/pallas_call | solution.py:432
  155.6 5.6 %shard_map.155 = f32[256,512]{1,0:T(8,128)} custom-call(s32[3]{0:T(128)S(1)} %pad_add_fusion.place, bf16[272,512]{1,0:T(8,128)(2,1)S(1)} %get-tuple-element.76.q_pack.refs_0_, bf16[272,512]{1,0:T(8,128)(2,1)S(1)} %get-tuple-element.92.do_pack.refs_1_, f32[256,128]{1,0:T(8,128)S(1)} %copy-done.29, f32[256,128]{1,0:T(8,128)S(1)} %get-tuple-element.94.delta_ref, ...), custom_call_target="tpu_custom_call" | custom-call | flops 1024 | bytes 1024 | tf_op jit(solution)/shard_map/pallas_call | solution.py:425
  161.2 2.6 %collective-permute-done.13 = bf16[64,4096]{1,0:T(8,128)(2,1)S(1)} collective-permute-done((bf16[64,4096]{1,0:T(8,128)(2,1)S(1)}, bf16[64,4096]{1,0:T(8,128)(2,1)S(1)}, u32[]{:S(2)}, u32[]{:S(2)}) %collective-permute-start.13) | collective-permute-done | bytes 524320 | tf_op jit(solution)/shard_map/ppermute | solution.py:56
  163.9 1.1 add_add_fusion
  165.0 2.8 %shard_map.157 = (f32[256,512]{1,0:T(8,128)}, f32[256,512]{1,0:T(8,128)}) custom-call(bf16[272,512]{1,0:T(8,128)(2,1)S(1)} %copy-done.25, bf16[272,512]{1,0:T(8,128)(2,1)S(1)} %collective-permute-done.17.refs_1_, bf16[272,512]{1,0:T(8,128)(2,1)S(1)} %collective-permute-done.18.refs_2_, bf16[272,512]{1,0:T(8,128)(2,1)S(1)} %collective-permute-done.19.refs_3_, ...), custom_call_target="tpu_custom_call" | custom-call | flops 1024 | bytes 1024 | tf_op jit(solution)/shard_map/pallas_call | solution.py:432
  (102 shorter events, 3.8 us)
Async XLA Ops:
  0.6 19.4 %copy-start = (bf16[256,4096]{1,0:T(8,128)(2,1)S(1)}, bf16[256,4096]{1,0:T(8,128)(2,1)}, u32[]{:S(2)}) copy-start(bf16[256,4096]{1,0:T(8,128)(2,1)} %param.14) | copy-start | bytes 6291460
  1.9 18.3 %collective-permute-start.1 = (bf16[2,256,512]{2,1,0:T(8,128)(2,1)S(1)}, bf16[2,256,512]{2,1,0:T(8,128)(2,1)S(1)}, u32[]{:S(2)}, u32[]{:S(2)}) collective-permute-start(bf16[2,256,512]{2,1,0:T(8,128)(2,1)S(1)} %pad_maximum_fusion.1), channel_id=1, source_target_pairs={{4,8},{12,16},{20,24},{28,32},{36,40},{44,48},{52,56},{60,64},{68,... | collective-permute-start | bytes 1572872 | tf_op jit(solution)/shard_map/ppermute | solution.py:66
  8.5 12.7 %collective-permute-start = (bf16[2,256,512]{2,1,0:T(8,128)(2,1)S(1)}, bf16[2,256,512]{2,1,0:T(8,128)(2,1)}, u32[]{:S(2)}, u32[]{:S(2)}) collective-permute-start(bf16[2,256,512]{2,1,0:T(8,128)(2,1)S(1)} %pad_maximum_fusion.1), channel_id=1, source_target_pairs={{0,4},{8,12},{16,20},{24,28},{32,36},{40,44},{48,52},{56,60},{64,6... | collective-permute-start | bytes 1572872 | tf_op jit(solution)/shard_map/ppermute | solution.py:66
  13.8 6.1 %copy-start.11 = (bf16[2,1,64,4096]{3,2,1,0:T(8,128)(2,1)}, bf16[2,1,64,4096]{3,2,1,0:T(8,128)(2,1)S(1)}, u32[]{:S(2)}) copy-start(bf16[2,1,64,4096]{3,2,1,0:T(8,128)(2,1)S(1)} %get-tuple-element.107) | copy-start | bytes 3145732
  21.2 16.7 %collective-permute-start.3 = (bf16[2,256,512]{2,1,0:T(8,128)(2,1)}, bf16[2,256,512]{2,1,0:T(8,128)(2,1)S(1)}, u32[]{:S(2)}, u32[]{:S(2)}) collective-permute-start(bf16[2,256,512]{2,1,0:T(8,128)(2,1)} %collective-permute-done.kv_a), channel_id=1, source_target_pairs={{4,8},{12,16},{20,24},{28,32},{36,40},{44,48},{52,56},{60,64},{68,... | collective-permute-start | bytes 1572872 | tf_op jit(solution)/shard_map/ppermute | solution.py:66
  26.2 11.7 %collective-permute-start.2 = (bf16[2,256,512]{2,1,0:T(8,128)(2,1)S(1)}, bf16[2,256,512]{2,1,0:T(8,128)(2,1)S(1)}, u32[]{:S(2)}, u32[]{:S(2)}) collective-permute-start(bf16[2,256,512]{2,1,0:T(8,128)(2,1)S(1)} %collective-permute-done.1.kv_b), channel_id=1, source_target_pairs={{0,4},{8,12},{16,20},{24,28},{32,36},{40,44},{48,52},{56,60},{64,6... | collective-permute-start | bytes 1572872 | tf_op jit(solution)/shard_map/ppermute | solution.py:66
  26.3 55.8 %slice-start = ((s8[8388608]{0:T(1024)(128)(4,1)}), s8[4194304]{0:T(1024)(128)(4,1)S(1)}, s32[]{:S(2)}) async-start(s8[8388608]{0:T(1024)(128)(4,1)} %bitcast.23), calls=%async_computation | async-start | bytes 8388608
  26.5 11.4 %copy-start.6 = (bf16[256,512]{1,0:T(8,128)(2,1)S(1)}, bf16[256,512]{1,0:T(8,128)(2,1)}, u32[]{:S(2)}) copy-start(bf16[256,512]{1,0:T(8,128)(2,1)} %refs_4_.1) | copy-start | bytes 786436
  26.5 11.4 %copy-start.7 = (bf16[256,512]{1,0:T(8,128)(2,1)S(1)}, bf16[256,512]{1,0:T(8,128)(2,1)}, u32[]{:S(2)}) copy-start(bf16[256,512]{1,0:T(8,128)(2,1)} %refs_5_.1) | copy-start | bytes 786436
  26.5 11.4 %copy-start.26 = (bf16[256,512]{1,0:T(8,128)(2,1)S(1)}, bf16[256,512]{1,0:T(8,128)(2,1)}, u32[]{:S(2)}) copy-start(bf16[256,512]{1,0:T(8,128)(2,1)} %q_ref.1) | copy-start | bytes 786436
  27.6 14.3 %copy-start.2 = (bf16[512,4096]{1,0:T(8,128)(2,1)S(1)}, bf16[512,4096]{1,0:T(8,128)(2,1)}, u32[]{:S(2)}) copy-start(bf16[512,4096]{1,0:T(8,128)(2,1)} %weight_ref.7) | copy-start | bytes 12582916
  37.8 5.4 %copy-start.13 = (bf16[2,256,512]{2,1,0:T(8,128)(2,1)}, bf16[2,256,512]{2,1,0:T(8,128)(2,1)S(1)}, u32[]{:S(2)}) copy-start(bf16[2,256,512]{2,1,0:T(8,128)(2,1)S(1)} %collective-permute-done.3.kv_d) | copy-start | bytes 1572868
  37.9 5.3 %copy-start.15 = (bf16[2,256,512]{2,1,0:T(8,128)(2,1)}, bf16[2,256,512]{2,1,0:T(8,128)(2,1)S(1)}, u32[]{:S(2)}) copy-start(bf16[2,256,512]{2,1,0:T(8,128)(2,1)S(1)} %collective-permute-done.2.kv_c) | copy-start | bytes 1572868
  37.9 44.3 %slice-start.1 = ((s8[8388608]{0:T(1024)(128)(4,1)}), s8[4194304]{0:T(1024)(128)(4,1)S(1)}, s32[]{:S(2)}) async-start(s8[8388608]{0:T(1024)(128)(4,1)} %bitcast.23), calls=%async_computation.1 | async-start | bytes 8388608
  43.3 31.4 %copy-start.27 = (f32[4096]{0:T(1024)S(1)}, f32[4096]{0:T(1024)}, u32[]{:S(2)}) copy-start(f32[4096]{0:T(1024)} %param.16) | copy-start | bytes 49156
  43.3 5.2 %collective-permute-start.4 = (bf16[128,4096]{1,0:T(8,128)(2,1)S(1)}, bf16[128,4096]{1,0:T(8,128)(2,1)S(1)}, u32[]{:S(2)}, u32[]{:S(2)}) collective-permute-start(bf16[128,4096]{1,0:T(8,128)(2,1)S(1)} %get-tuple-element.62), channel_id=1, source_target_pairs={{0,1},{1,0},{2,3},{3,2},{4,5},{5,4},{6,7},{7,6},{8,9},{9,8},{10,11... | collective-permute-start | bytes 3145736 | tf_op jit(solution)/shard_map/ppermute | solution.py:52
  48.7 33.5 %copy-start.5 = (bf16[1024,1024]{1,0:T(8,128)(2,1)S(1)}, bf16[1024,1024]{1,0:T(8,128)(2,1)}, u32[]{:S(2)}) copy-start(bf16[1024,1024]{1,0:T(8,128)(2,1)} %fusion.2.pick_ref) | copy-start | bytes 6291460
  48.7 26.0 %collective-permute-start.5 = (bf16[128,4096]{1,0:T(8,128)(2,1)S(1)}, bf16[128,4096]{1,0:T(8,128)(2,1)S(1)}, u32[]{:S(2)}, u32[]{:S(2)}) collective-permute-start(bf16[128,4096]{1,0:T(8,128)(2,1)S(1)} %add_convert_fusion.1.near_ref), channel_id=1, source_target_pairs={{0,2},{2,0},{1,3},{3,1},{4,6},{6,4},{5,7},{7,5},{8,10},{10,8},{9,1... | collective-permute-start | bytes 3145736 | tf_op jit(solution)/shard_map/ppermute | solution.py:56
  51.4 7.5 %collective-permute-start.6 = (bf16[272,512]{1,0:T(8,128)(2,1)S(1)}, bf16[272,512]{1,0:T(8,128)(2,1)S(1)}, u32[]{:S(2)}, u32[]{:S(2)}) collective-permute-start(bf16[272,512]{1,0:T(8,128)(2,1)S(1)} %get-tuple-element.76.q_pack.refs_0_), channel_id=1, source_target_pairs={{0,4},{8,12},{16,20},{24,28},{32,36},{40,44},{48,52},{56,60},{64,6... | collective-permute-start | bytes 835592 | tf_op jit(solution)/shard_map/ppermute | solution.py:66
  58.9 28.1 %copy-start.19 = (bf16[272,512]{1,0:T(8,128)(2,1)}, bf16[272,512]{1,0:T(8,128)(2,1)S(1)}, u32[]{:S(2)}) copy-start(bf16[272,512]{1,0:T(8,128)(2,1)S(1)} %collective-permute-done.6.refs_2_) | copy-start | bytes 835588
  74.7 12.4 %slice-start.2 = ((s8[8388608]{0:T(1024)(128)(4,1)}), s8[4194304]{0:T(1024)(128)(4,1)S(1)}, s32[]{:S(2)}) async-start(s8[8388608]{0:T(1024)(128)(4,1)} %bitcast.25), calls=%async_computation.2 | async-start | bytes 8388608
  75.8 11.2 %copy-start.8 = (f32[128,4096]{1,0:T(8,128)}, f32[128,4096]{1,0:T(8,128)S(1)}, u32[]{:S(2)}) copy-start(f32[128,4096]{1,0:T(8,128)S(1)} %get-tuple-element.67.unit_ref) | copy-start | bytes 6291460
  75.8 6.3 %collective-permute-start.7 = (bf16[128,4096]{1,0:T(8,128)(2,1)S(1)}, bf16[128,4096]{1,0:T(8,128)(2,1)S(1)}, u32[]{:S(2)}, u32[]{:S(2)}) collective-permute-start(bf16[128,4096]{1,0:T(8,128)(2,1)S(1)} %get-tuple-element.68.own_ref), channel_id=1, source_target_pairs={{0,1},{1,0},{2,3},{3,2},{4,5},{5,4},{6,7},{7,6},{8,9},{9,8},{10,11... | collective-permute-start | bytes 3145736 | tf_op jit(solution)/shard_map/ppermute | solution.py:52
  77.1 13.3 %collective-permute-start.8 = (bf16[272,512]{1,0:T(8,128)(2,1)S(1)}, bf16[272,512]{1,0:T(8,128)(2,1)S(1)}, u32[]{:S(2)}, u32[]{:S(2)}) collective-permute-start(bf16[272,512]{1,0:T(8,128)(2,1)S(1)} %get-tuple-element.76.q_pack.refs_0_), channel_id=1, source_target_pairs={{4,8},{12,16},{20,24},{28,32},{36,40},{44,48},{52,56},{60,64},{68,... | collective-permute-start | bytes 835592 | tf_op jit(solution)/shard_map/ppermute | solution.py:66
  82.2 4.9 %slice-start.3 = ((s8[8388608]{0:T(1024)(128)(4,1)}), s8[4194304]{0:T(1024)(128)(4,1)S(1)}, s32[]{:S(2)}) async-start(s8[8388608]{0:T(1024)(128)(4,1)} %bitcast.25), calls=%async_computation.3 | async-start | bytes 8388608
  93.7 3.3 %collective-permute-start.9 = (bf16[128,4096]{1,0:T(8,128)(2,1)}, bf16[128,4096]{1,0:T(8,128)(2,1)}, u32[]{:S(2)}, u32[]{:S(2)}) collective-permute-start(bf16[128,4096]{1,0:T(8,128)(2,1)} %get-tuple-element.79), channel_id=1, source_target_pairs={{0,1},{1,0},{2,3},{3,2},{4,5},{5,4},{6,7},{7,6},{8,9},{9,8},{10,11... | collective-permute-start | bytes 3145736 | tf_op jit(solution)/shard_map/ppermute | solution.py:52
  94.4 6.8 %collective-permute-start.11 = (bf16[128,4096]{1,0:T(8,128)(2,1)}, bf16[128,4096]{1,0:T(8,128)(2,1)}, u32[]{:S(2)}, u32[]{:S(2)}) collective-permute-start(bf16[128,4096]{1,0:T(8,128)(2,1)} %get-tuple-element.81), channel_id=1, source_target_pairs={{0,1},{1,0},{2,3},{3,2},{4,5},{5,4},{6,7},{7,6},{8,9},{9,8},{10,11... | collective-permute-start | bytes 3145736 | tf_op jit(solution)/shard_map/ppermute | solution.py:52
  94.4 6.8 %copy-start.22 = (bf16[272,512]{1,0:T(8,128)(2,1)S(1)}, bf16[272,512]{1,0:T(8,128)(2,1)}, u32[]{:S(2)}) copy-start(bf16[272,512]{1,0:T(8,128)(2,1)} %copy-done.21) | copy-start | bytes 835588
  98.5 26.0 %collective-permute-start.10 = (bf16[128,4096]{1,0:T(8,128)(2,1)S(1)}, bf16[128,4096]{1,0:T(8,128)(2,1)S(1)}, u32[]{:S(2)}, u32[]{:S(2)}) collective-permute-start(bf16[128,4096]{1,0:T(8,128)(2,1)S(1)} %add_convert_fusion.near_ref), channel_id=1, source_target_pairs={{0,2},{2,0},{1,3},{3,1},{4,6},{6,4},{5,7},{7,5},{8,10},{10,8},{9,1... | collective-permute-start | bytes 3145736 | tf_op jit(solution)/shard_map/ppermute | solution.py:56
  101.2 7.5 %collective-permute-start.12 = (bf16[272,512]{1,0:T(8,128)(2,1)S(1)}, bf16[272,512]{1,0:T(8,128)(2,1)S(1)}, u32[]{:S(2)}, u32[]{:S(2)}) collective-permute-start(bf16[272,512]{1,0:T(8,128)(2,1)S(1)} %copy-done.22), channel_id=1, source_target_pairs={{0,4},{8,12},{16,20},{24,28},{32,36},{40,44},{48,52},{56,60},{64,6... | collective-permute-start | bytes 835592 | tf_op jit(solution)/shard_map/ppermute | solution.py:66
  102.7 21.8 %copy-start.9 = (f32[128,4096]{1,0:T(8,128)S(1)}, f32[128,4096]{1,0:T(8,128)}, u32[]{:S(2)}) copy-start(f32[128,4096]{1,0:T(8,128)} %copy-done.8) | copy-start | bytes 6291460
  102.7 21.8 %copy-start.12 = (bf16[2,1,64,4096]{3,2,1,0:T(8,128)(2,1)S(1)}, bf16[2,1,64,4096]{3,2,1,0:T(8,128)(2,1)}, u32[]{:S(2)}) copy-start(bf16[2,1,64,4096]{3,2,1,0:T(8,128)(2,1)} %copy-done.11) | copy-start | bytes 3145732
  108.8 17.0 %copy-start.24 = (bf16[272,512]{1,0:T(8,128)(2,1)}, bf16[272,512]{1,0:T(8,128)(2,1)S(1)}, u32[]{:S(2)}) copy-start(bf16[272,512]{1,0:T(8,128)(2,1)S(1)} %collective-permute-done.12.refs_0_) | copy-start | bytes 835588
  125.8 7.7 %collective-permute-start.14 = (bf16[128,4096]{1,0:T(8,128)(2,1)S(1)}, bf16[128,4096]{1,0:T(8,128)(2,1)S(1)}, u32[]{:S(2)}, u32[]{:S(2)}) collective-permute-start(bf16[128,4096]{1,0:T(8,128)(2,1)S(1)} %shard_map.152.low_ref), channel_id=1, source_target_pairs={{0,1},{1,0},{2,3},{3,2},{4,5},{5,4},{6,7},{7,6},{8,9},{9,8},{10,11... | collective-permute-start | bytes 3145736 | tf_op jit(solution)/shard_map/ppermute | solution.py:52
  129.3 4.2 %copy-start.4 = (bf16[512,4096]{1,0:T(8,128)(2,1)S(1)}, bf16[512,4096]{1,0:T(8,128)(2,1)}, u32[]{:S(2)}) copy-start(bf16[512,4096]{1,0:T(8,128)(2,1)} %weight_ref.7) | copy-start | bytes 12582916
  129.3 4.2 %copy-start.18 = (bf16[256,512]{1,0:T(8,128)(2,1)S(1)}, bf16[256,512]{1,0:T(8,128)(2,1)}, u32[]{:S(2)}) copy-start(bf16[256,512]{1,0:T(8,128)(2,1)} %copy-done.17) | copy-start | bytes 786436
  130.8 33.0 %collective-permute-start.13 = (bf16[64,4096]{1,0:T(8,128)(2,1)S(1)}, bf16[64,4096]{1,0:T(8,128)(2,1)S(1)}, u32[]{:S(2)}, u32[]{:S(2)}) collective-permute-start(bf16[64,4096]{1,0:T(8,128)(2,1)S(1)} %copy-done.32), channel_id=1, source_target_pairs={{0,2},{2,0},{1,3},{3,1},{4,6},{6,4},{5,7},{7,5},{8,10},{10,8},{9,1... | collective-permute-start | bytes 1572872 | tf_op jit(solution)/shard_map/ppermute | solution.py:56
  135.2 12.9 %collective-permute-start.16 = (bf16[272,512]{1,0:T(8,128)(2,1)S(1)}, bf16[272,512]{1,0:T(8,128)(2,1)S(1)}, u32[]{:S(2)}, u32[]{:S(2)}) collective-permute-start(bf16[272,512]{1,0:T(8,128)(2,1)S(1)} %get-tuple-element.92.do_pack.refs_1_), channel_id=1, source_target_pairs={{4,8},{12,16},{20,24},{28,32},{36,40},{44,48},{52,56},{60,64},{68,... | collective-permute-start | bytes 835592 | tf_op jit(solution)/shard_map/ppermute | solution.py:66
  139.7 8.4 %collective-permute-start.15 = (bf16[272,512]{1,0:T(8,128)(2,1)S(1)}, bf16[272,512]{1,0:T(8,128)(2,1)S(1)}, u32[]{:S(2)}, u32[]{:S(2)}) collective-permute-start(bf16[272,512]{1,0:T(8,128)(2,1)S(1)} %get-tuple-element.92.do_pack.refs_1_), channel_id=1, source_target_pairs={{0,4},{8,12},{16,20},{24,28},{32,36},{40,44},{48,52},{56,60},{64,6... | collective-permute-start | bytes 835592 | tf_op jit(solution)/shard_map/ppermute | solution.py:66
  140.1 12.8 %copy-start.23 = (bf16[272,512]{1,0:T(8,128)(2,1)S(1)}, bf16[272,512]{1,0:T(8,128)(2,1)}, u32[]{:S(2)}) copy-start(bf16[272,512]{1,0:T(8,128)(2,1)} %copy-done.21) | copy-start | bytes 835588
  141.1 14.5 %copy-start.14 = (bf16[2,256,512]{2,1,0:T(8,128)(2,1)S(1)}, bf16[2,256,512]{2,1,0:T(8,128)(2,1)}, u32[]{:S(2)}) copy-start(bf16[2,256,512]{2,1,0:T(8,128)(2,1)} %copy-done.13) | copy-start | bytes 1572868
  141.1 14.5 %copy-start.16 = (bf16[2,256,512]{2,1,0:T(8,128)(2,1)S(1)}, bf16[2,256,512]{2,1,0:T(8,128)(2,1)}, u32[]{:S(2)}) copy-start(bf16[2,256,512]{2,1,0:T(8,128)(2,1)} %copy-done.15) | copy-start | bytes 1572868
  141.1 14.5 %copy-start.29 = (f32[256,128]{1,0:T(8,128)S(1)}, f32[256,128]{1,0:T(8,128)}, u32[]{:S(2)}) copy-start(f32[256,128]{1,0:T(8,128)} %copy-done.28) | copy-start | bytes 393220
  141.1 23.9 %collective-permute-start.18 = (bf16[272,512]{1,0:T(8,128)(2,1)S(1)}, bf16[272,512]{1,0:T(8,128)(2,1)S(1)}, u32[]{:S(2)}, u32[]{:S(2)}) collective-permute-start(bf16[272,512]{1,0:T(8,128)(2,1)S(1)} %copy-done.20), channel_id=1, source_target_pairs={{4,8},{12,16},{20,24},{28,32},{36,40},{44,48},{52,56},{60,64},{68,... | collective-permute-start | bytes 835592 | tf_op jit(solution)/shard_map/ppermute | solution.py:66
  148.1 16.9 %collective-permute-start.19 = (bf16[272,512]{1,0:T(8,128)(2,1)S(1)}, bf16[272,512]{1,0:T(8,128)(2,1)S(1)}, u32[]{:S(2)}, u32[]{:S(2)}) collective-permute-start(bf16[272,512]{1,0:T(8,128)(2,1)S(1)} %collective-permute-done.15.refs_3_), channel_id=1, source_target_pairs={{4,8},{12,16},{20,24},{28,32},{36,40},{44,48},{52,56},{60,64},{68,... | collective-permute-start | bytes 835592 | tf_op jit(solution)/shard_map/ppermute | solution.py:66
  152.5 12.5 %collective-permute-start.17 = (bf16[272,512]{1,0:T(8,128)(2,1)S(1)}, bf16[272,512]{1,0:T(8,128)(2,1)S(1)}, u32[]{:S(2)}, u32[]{:S(2)}) collective-permute-start(bf16[272,512]{1,0:T(8,128)(2,1)S(1)} %collective-permute-done.16.refs_5_), channel_id=1, source_target_pairs={{0,4},{8,12},{16,20},{24,28},{32,36},{40,44},{48,52},{56,60},{64,6... | collective-permute-start | bytes 835592 | tf_op jit(solution)/shard_map/ppermute | solution.py:66
  155.6 8.3 %copy-start.10 = (f32[128,4096]{1,0:T(8,128)S(1)}, f32[128,4096]{1,0:T(8,128)}, u32[]{:S(2)}) copy-start(f32[128,4096]{1,0:T(8,128)} %copy-done.8) | copy-start | bytes 6291460
  155.6 8.3 %copy-start.31 = (f32[64,4096]{1,0:T(8,128)S(1)}, f32[64,4096]{1,0:T(8,128)}, u32[]{:S(2)}) copy-start(f32[64,4096]{1,0:T(8,128)} %slice_select_fusion) | copy-start | bytes 3145732
  (9 other events, 19.6 us)
